TPU v7x, 32 devices: a whole 2x2x4 slice. The times are simulated.
32 devices in a mesh: section: 4 (over z), seq: 8 (over y, x, core).
Axes of the slice: x: 2, y: 2, z: 4, core: 2. Of those that a mesh axis runs over, the one named last changes fastest.
Arguments:
- bases: int32 [4, 262144], P(None, 'seq'), may hold values from 0 to 3
- stem_weight: bfloat16 [512, 1536], replicated, may hold values from -0.5 to 0.5
- norm_gain: float32 [4, 1536], P('section'), may hold values from 0.25 to 1.75
- conv_taps: float32 [4, 5, 1536], P('section'), may hold values from -2.7 to 2.7
- proj_weight: bfloat16 [4, 1536, 1536], P('section'), may hold values from -0.15625 to 0.15625
- dest: int32 [256], P('seq'), may hold values from 0 to 255, as said below
Outputs:
- hints: bfloat16 [4, 4, 2048, 1536], P('section', None, 'seq')
Inputs may be any that keep to these rules, and one draw needn't show every extreme that they name: dest is a permutation. Slot dest[r] belongs to owner dest[r] // 32; the runs of one index d of seq (r from d * 32) go to every owner in equal numbers, 4 each, and (dest[r] % 32) // 4 equals d.
All inputs are finite; a program needn't handle non-finite values.
Results may differ from a plain program's by a relative error of at most 0.007.
Values may be sent and summed in bfloat16 or wider, within the bound.
A program may use at most 64 MiB of HBM per device.

v0:
```python
import jax
import jax.numpy as jnp
from jax import lax
from jax.sharding import PartitionSpec as P

BLOCK_BP = 128


def extended(block, sides, width):
    for axis, dim in sides:
        count = lax.axis_size(axis)
        forward = [(i, i + 1) for i in range(count - 1)]
        backward = [(target, source) for source, target in forward]
        low = lax.ppermute(
            lax.slice_in_dim(block, block.shape[dim] - width, None, axis=dim), axis, forward
        )
        high = lax.ppermute(lax.slice_in_dim(block, 0, width, axis=dim), axis, backward)
        block = jnp.concatenate([low, block, high], axis=dim)
    return block


def passed_along(value, axis, steps):
    count = lax.axis_size(axis)
    initial, last = (max(0, -steps), min(count, count - steps))
    return lax.ppermute(value, axis, [(source, source + steps) for source in range(initial, last)])


def section_block(current, gain_row, tap_rows, weight):
    wide_state = current.astype(jnp.float32)
    inv_rms = lax.rsqrt(jnp.mean(wide_state * wide_state, axis=-1, keepdims=True) + 1e-06)
    normed = (wide_state * inv_rms * gain_row).astype(jnp.bfloat16)
    reach = tap_rows.shape[0] // 2
    padded = extended(normed, (("seq", 0),), reach)
    length = current.shape[0]
    mixed = jnp.zeros(current.shape, jnp.float32)
    for offset in range(tap_rows.shape[0]):
        mixed = mixed + tap_rows[offset] * padded[offset : offset + length].astype(jnp.float32)
    mixed = mixed.astype(jnp.bfloat16)
    update = jnp.dot(mixed, weight, preferred_element_type=jnp.float32)
    return (wide_state + jax.nn.gelu(update)).astype(jnp.bfloat16)


def on_device(bases, stem_weight, norm_gain, conv_taps, proj_weight, dest):
    micro_count = bases.shape[0]
    row_count = bases.shape[1] // BLOCK_BP
    channels = stem_weight.shape[1]
    section_count = lax.axis_size("section")
    section_id = lax.axis_index("section")
    segs_dev = dest.shape[0]
    per_peer = segs_dev // lax.axis_size("seq")
    seg_rows = row_count // segs_dev
    base_codes = bases.reshape(micro_count * row_count, BLOCK_BP)
    onehot = (base_codes[:, :, None] == jnp.arange(4, dtype=jnp.int32)).astype(jnp.bfloat16)
    onehot = onehot.reshape(micro_count * row_count, BLOCK_BP * 4)
    embedded = jnp.dot(onehot, stem_weight, preferred_element_type=jnp.float32).astype(jnp.bfloat16)
    embedded = embedded.reshape(micro_count, row_count, channels)
    gain_row = norm_gain[0]
    tap_rows = conv_taps[0]
    weight = proj_weight[0]
    send_slot = dest // segs_dev * per_peer + dest % segs_dev % per_peer
    select = (send_slot[None, :] == jnp.arange(segs_dev, dtype=jnp.int32)[:, None]).astype(
        jnp.bfloat16
    )

    def arrange(current):
        grouped = current.reshape(segs_dev, seg_rows * channels)
        ordered = jnp.dot(select, grouped, preferred_element_type=jnp.float32).astype(jnp.bfloat16)
        return ordered.reshape(row_count, channels)

    def advance(moment, carried):
        incoming, hint_rows = carried
        entering = lax.dynamic_index_in_dim(
            embedded, jnp.clip(moment, 0, micro_count - 1), 0, keepdims=False
        )
        current = jnp.where(section_id == 0, entering, incoming)
        leaving = section_block(current, gain_row, tap_rows, weight)
        micro_idx = moment - section_id
        slot_idx = jnp.clip(micro_idx, 0, micro_count - 1)
        in_range = (micro_idx >= 0) & (micro_idx < micro_count)
        arrived = lax.all_to_all(arrange(leaving), "seq", split_axis=0, concat_axis=0, tiled=True)
        previous = lax.dynamic_index_in_dim(hint_rows, slot_idx, 0, keepdims=False)
        arrived = jnp.where(in_range, arrived, previous)
        hint_rows = lax.dynamic_update_index_in_dim(hint_rows, arrived, slot_idx, 0)
        incoming = passed_along(leaving, "section", 1)
        return (incoming, hint_rows)

    start_state = jnp.zeros((row_count, channels), jnp.bfloat16)
    start_hints = jnp.zeros((micro_count, row_count, channels), jnp.bfloat16)
    final_state, hint_rows = lax.fori_loop(
        0, micro_count + section_count - 1, advance, (start_state, start_hints)
    )
    return hint_rows[None]


def solution(mesh):
    return jax.shard_map(
        on_device,
        mesh=mesh,
        in_specs=(
            P(None, "seq"),
            P(),
            P("section", None),
            P("section", None, None),
            P("section", None, None),
            P("seq"),
        ),
        out_specs=P("section", None, "seq", None),
        check_vma=False,
    )
```

profile of v0, /device:TPU:0, one launch (start us, length us, event | category | flops | bytes accessed | tf_op | source)
XLA Modules:
  0.0 320.2 jit_solution(564011685951406488)
XLA Ops:
  3.3 1.9 eq.49
  5.2 3.0 eq.50
  8.2 5.2 %convolution_convert_fusion.1 = bf16[1024,1536]{1,0:T(8,128)(2,1)} fusion(bf16[512,1536]{1,0:T(8,128)(2,1)S(1)} %copy-done, s32[1024,512]{0,1:T(8,128)} %eq.50, s32[512]{0:T(512)S(1)} %eq.52), kind=kOutput, calls=%fused_computation.48 | convolution fusion | flops 1612709888 | bytes 6817792 | tf_op jit(solution)/shard_map/dot_general | solution.py:55
  13.4 1.9 broadcast_in_dim.20
  15.3 304.9 %while.17 = (s32[]{:T(128)}, bf16[256,1536]{1,0:T(8,128)(2,1)S(1)}, bf16[4,256,1536]{2,1,0:T(8,128)(2,1)}, pred[]{:T(512)}, bf16[4,256,1536]{2,1,0:T(8,128)(2,1)...) while((s32[]{:T(128)}, bf16[256,1536]{1,0:T(8,128)(2,1)S(1)}, ...), condition=%wide.region_2.3_spmd.clone, body=%wide.region_0.2_spmd.clone.sunk | while | flops 1252002048 | bytes 23794180 | solution.py:89
  15.3 1.5 fusion.49
  18.4 3.0 collective-permute-start.1
  22.3 5.4 %fusion.52 = bf16[256,1536]{1,0:T(8,128)(2,1)} fusion(bf16[256,1536]{1,0:T(8,128)(2,1)S(1)} %get-tuple-element.323, bf16[1536,1536]{1,0:T(8,128)(2,1)} %get-tuple-element.369, bf16[256,1536]{1,0:T(8,128)(2,1)S(1)} %fusion.50, bf16[2,1536]{1,0:T(2,128)(2,1)S(1)} %collective-permute-done, bf16[2,1536]{1,0:T(2,128)(2,1)S(1)} %collective-permute-done.1, ...), kind=kOutput, calls=%fused_computation.10.clone.1 | convolution fusion | flops 1222901760 | bytes 7120896 | tf_op jit(solution)/shard_map/while/body/eval_jaxpr/dot_general | solution.py:39
  27.7 1.5 reshape.49
  30.7 7.7 %all-to-all-start = ((bf16[8,32,1536]{2,1,0:T(8,128)(2,1)}), bf16[8,32,1536]{2,1,0:T(8,128)(2,1)S(1)}, u32[]{:S(2)}, u32[]{:S(2)}) async-start(bf16[8,32,1536]{2,1,0:T(8,128)(2,1)} %all_to_all.18), calls=%async_computation | async-start | bytes 1572864 | tf_op jit(solution)/shard_map/while/body/eval_jaxpr/all_to_all | solution.py:80
  38.5 3.5 %collective-permute-start.2 = (bf16[256,1536]{1,0:T(8,128)(2,1)}, bf16[256,1536]{1,0:T(8,128)(2,1)S(1)}, u32[]{:S(2)}, u32[]{:S(2)}) collective-permute-start(bf16[256,1536]{1,0:T(8,128)(2,1)} %fusion.52), channel_id=1, source_target_pairs={{0,8},{8,16},{16,24},{1,9},{9,17},{17,25},{2,10},{10,18},{18,26},{... | collective-permute-start | bytes 2359304 | tf_op jit(solution)/shard_map/while/body/eval_jaxpr/ppermute | solution.py:25
  42.0 9.1 %all-to-all-done = bf16[8,32,1536]{2,1,0:T(8,128)(2,1)S(1)} async-done(((bf16[8,32,1536]{2,1,0:T(8,128)(2,1)}), bf16[8,32,1536]{2,1,0:T(8,128)(2,1)S(1)}, u32[]{:S(2)}, u32[]{:S(2)}) %all-to-all-start) | async-done | bytes 786464 | tf_op jit(solution)/shard_map/while/body/eval_jaxpr/all_to_all | solution.py:80
  51.1 2.2 fusion.54
  53.3 6.4 %collective-permute-done.2 = bf16[256,1536]{1,0:T(8,128)(2,1)S(1)} collective-permute-done((bf16[256,1536]{1,0:T(8,128)(2,1)}, bf16[256,1536]{1,0:T(8,128)(2,1)S(1)}, u32[]{:S(2)}, u32[]{:S(2)}) %collective-permute-start.2) | collective-permute-done | bytes 786464 | tf_op jit(solution)/shard_map/while/body/eval_jaxpr/ppermute | solution.py:25
  59.7 1.5 fusion.49
  62.8 3.0 collective-permute-start.1
  66.7 5.4 %fusion.52 = bf16[256,1536]{1,0:T(8,128)(2,1)} fusion(bf16[256,1536]{1,0:T(8,128)(2,1)S(1)} %get-tuple-element.323, bf16[1536,1536]{1,0:T(8,128)(2,1)} %get-tuple-element.369, bf16[256,1536]{1,0:T(8,128)(2,1)S(1)} %fusion.50, bf16[2,1536]{1,0:T(2,128)(2,1)S(1)} %collective-permute-done, bf16[2,1536]{1,0:T(2,128)(2,1)S(1)} %collective-permute-done.1, ...), kind=kOutput, calls=%fused_computation.10.clone.1 | convolution fusion | flops 1222901760 | bytes 7120896 | tf_op jit(solution)/shard_map/while/body/eval_jaxpr/dot_general | solution.py:39
  75.1 5.9 %all-to-all-start = ((bf16[8,32,1536]{2,1,0:T(8,128)(2,1)}), bf16[8,32,1536]{2,1,0:T(8,128)(2,1)S(1)}, u32[]{:S(2)}, u32[]{:S(2)}) async-start(bf16[8,32,1536]{2,1,0:T(8,128)(2,1)} %all_to_all.18), calls=%async_computation | async-start | bytes 1572864 | tf_op jit(solution)/shard_map/while/body/eval_jaxpr/all_to_all | solution.py:80
  81.1 4.3 %collective-permute-start.2 = (bf16[256,1536]{1,0:T(8,128)(2,1)}, bf16[256,1536]{1,0:T(8,128)(2,1)S(1)}, u32[]{:S(2)}, u32[]{:S(2)}) collective-permute-start(bf16[256,1536]{1,0:T(8,128)(2,1)} %fusion.52), channel_id=1, source_target_pairs={{0,8},{8,16},{16,24},{1,9},{9,17},{17,25},{2,10},{10,18},{18,26},{... | collective-permute-start | bytes 2359304 | tf_op jit(solution)/shard_map/while/body/eval_jaxpr/ppermute | solution.py:25
  85.4 8.3 %all-to-all-done = bf16[8,32,1536]{2,1,0:T(8,128)(2,1)S(1)} async-done(((bf16[8,32,1536]{2,1,0:T(8,128)(2,1)}), bf16[8,32,1536]{2,1,0:T(8,128)(2,1)S(1)}, u32[]{:S(2)}, u32[]{:S(2)}) %all-to-all-start) | async-done | bytes 786464 | tf_op jit(solution)/shard_map/while/body/eval_jaxpr/all_to_all | solution.py:80
  93.7 2.2 fusion.54
  95.9 7.2 %collective-permute-done.2 = bf16[256,1536]{1,0:T(8,128)(2,1)S(1)} collective-permute-done((bf16[256,1536]{1,0:T(8,128)(2,1)}, bf16[256,1536]{1,0:T(8,128)(2,1)S(1)}, u32[]{:S(2)}, u32[]{:S(2)}) %collective-permute-start.2) | collective-permute-done | bytes 786464 | tf_op jit(solution)/shard_map/while/body/eval_jaxpr/ppermute | solution.py:25
  103.1 1.5 fusion.49
  106.2 3.0 collective-permute-start.1
  110.1 5.4 %fusion.52 = bf16[256,1536]{1,0:T(8,128)(2,1)} fusion(bf16[256,1536]{1,0:T(8,128)(2,1)S(1)} %get-tuple-element.323, bf16[1536,1536]{1,0:T(8,128)(2,1)} %get-tuple-element.369, bf16[256,1536]{1,0:T(8,128)(2,1)S(1)} %fusion.50, bf16[2,1536]{1,0:T(2,128)(2,1)S(1)} %collective-permute-done, bf16[2,1536]{1,0:T(2,128)(2,1)S(1)} %collective-permute-done.1, ...), kind=kOutput, calls=%fused_computation.10.clone.1 | convolution fusion | flops 1222901760 | bytes 7120896 | tf_op jit(solution)/shard_map/while/body/eval_jaxpr/dot_general | solution.py:39
  115.5 1.5 reshape.49
  118.6 5.9 %all-to-all-start = ((bf16[8,32,1536]{2,1,0:T(8,128)(2,1)}), bf16[8,32,1536]{2,1,0:T(8,128)(2,1)S(1)}, u32[]{:S(2)}, u32[]{:S(2)}) async-start(bf16[8,32,1536]{2,1,0:T(8,128)(2,1)} %all_to_all.18), calls=%async_computation | async-start | bytes 1572864 | tf_op jit(solution)/shard_map/while/body/eval_jaxpr/all_to_all | solution.py:80
  124.5 4.3 %collective-permute-start.2 = (bf16[256,1536]{1,0:T(8,128)(2,1)}, bf16[256,1536]{1,0:T(8,128)(2,1)S(1)}, u32[]{:S(2)}, u32[]{:S(2)}) collective-permute-start(bf16[256,1536]{1,0:T(8,128)(2,1)} %fusion.52), channel_id=1, source_target_pairs={{0,8},{8,16},{16,24},{1,9},{9,17},{17,25},{2,10},{10,18},{18,26},{... | collective-permute-start | bytes 2359304 | tf_op jit(solution)/shard_map/while/body/eval_jaxpr/ppermute | solution.py:25
  128.8 8.3 %all-to-all-done = bf16[8,32,1536]{2,1,0:T(8,128)(2,1)S(1)} async-done(((bf16[8,32,1536]{2,1,0:T(8,128)(2,1)}), bf16[8,32,1536]{2,1,0:T(8,128)(2,1)S(1)}, u32[]{:S(2)}, u32[]{:S(2)}) %all-to-all-start) | async-done | bytes 786464 | tf_op jit(solution)/shard_map/while/body/eval_jaxpr/all_to_all | solution.py:80
  137.1 2.2 fusion.54
  139.3 7.2 %collective-permute-done.2 = bf16[256,1536]{1,0:T(8,128)(2,1)S(1)} collective-permute-done((bf16[256,1536]{1,0:T(8,128)(2,1)}, bf16[256,1536]{1,0:T(8,128)(2,1)S(1)}, u32[]{:S(2)}, u32[]{:S(2)}) %collective-permute-start.2) | collective-permute-done | bytes 786464 | tf_op jit(solution)/shard_map/while/body/eval_jaxpr/ppermute | solution.py:25
  146.6 1.5 fusion.49
  149.7 3.0 collective-permute-start.1
  153.5 5.4 %fusion.52 = bf16[256,1536]{1,0:T(8,128)(2,1)} fusion(bf16[256,1536]{1,0:T(8,128)(2,1)S(1)} %get-tuple-element.323, bf16[1536,1536]{1,0:T(8,128)(2,1)} %get-tuple-element.369, bf16[256,1536]{1,0:T(8,128)(2,1)S(1)} %fusion.50, bf16[2,1536]{1,0:T(2,128)(2,1)S(1)} %collective-permute-done, bf16[2,1536]{1,0:T(2,128)(2,1)S(1)} %collective-permute-done.1, ...), kind=kOutput, calls=%fused_computation.10.clone.1 | convolution fusion | flops 1222901760 | bytes 7120896 | tf_op jit(solution)/shard_map/while/body/eval_jaxpr/dot_general | solution.py:39
  158.9 1.5 reshape.49
  162.0 5.9 %all-to-all-start = ((bf16[8,32,1536]{2,1,0:T(8,128)(2,1)}), bf16[8,32,1536]{2,1,0:T(8,128)(2,1)S(1)}, u32[]{:S(2)}, u32[]{:S(2)}) async-start(bf16[8,32,1536]{2,1,0:T(8,128)(2,1)} %all_to_all.18), calls=%async_computation | async-start | bytes 1572864 | tf_op jit(solution)/shard_map/while/body/eval_jaxpr/all_to_all | solution.py:80
  167.9 4.3 %collective-permute-start.2 = (bf16[256,1536]{1,0:T(8,128)(2,1)}, bf16[256,1536]{1,0:T(8,128)(2,1)S(1)}, u32[]{:S(2)}, u32[]{:S(2)}) collective-permute-start(bf16[256,1536]{1,0:T(8,128)(2,1)} %fusion.52), channel_id=1, source_target_pairs={{0,8},{8,16},{16,24},{1,9},{9,17},{17,25},{2,10},{10,18},{18,26},{... | collective-permute-start | bytes 2359304 | tf_op jit(solution)/shard_map/while/body/eval_jaxpr/ppermute | solution.py:25
  172.3 8.3 %all-to-all-done = bf16[8,32,1536]{2,1,0:T(8,128)(2,1)S(1)} async-done(((bf16[8,32,1536]{2,1,0:T(8,128)(2,1)}), bf16[8,32,1536]{2,1,0:T(8,128)(2,1)S(1)}, u32[]{:S(2)}, u32[]{:S(2)}) %all-to-all-start) | async-done | bytes 786464 | tf_op jit(solution)/shard_map/while/body/eval_jaxpr/all_to_all | solution.py:80
  180.5 2.2 fusion.54
  182.7 7.2 %collective-permute-done.2 = bf16[256,1536]{1,0:T(8,128)(2,1)S(1)} collective-permute-done((bf16[256,1536]{1,0:T(8,128)(2,1)}, bf16[256,1536]{1,0:T(8,128)(2,1)S(1)}, u32[]{:S(2)}, u32[]{:S(2)}) %collective-permute-start.2) | collective-permute-done | bytes 786464 | tf_op jit(solution)/shard_map/while/body/eval_jaxpr/ppermute | solution.py:25
  190.0 1.5 fusion.49
  193.1 3.0 collective-permute-start.1
  196.9 5.4 %fusion.52 = bf16[256,1536]{1,0:T(8,128)(2,1)} fusion(bf16[256,1536]{1,0:T(8,128)(2,1)S(1)} %get-tuple-element.323, bf16[1536,1536]{1,0:T(8,128)(2,1)} %get-tuple-element.369, bf16[256,1536]{1,0:T(8,128)(2,1)S(1)} %fusion.50, bf16[2,1536]{1,0:T(2,128)(2,1)S(1)} %collective-permute-done, bf16[2,1536]{1,0:T(2,128)(2,1)S(1)} %collective-permute-done.1, ...), kind=kOutput, calls=%fused_computation.10.clone.1 | convolution fusion | flops 1222901760 | bytes 7120896 | tf_op jit(solution)/shard_map/while/body/eval_jaxpr/dot_general | solution.py:39
  205.4 5.9 %all-to-all-start = ((bf16[8,32,1536]{2,1,0:T(8,128)(2,1)}), bf16[8,32,1536]{2,1,0:T(8,128)(2,1)S(1)}, u32[]{:S(2)}, u32[]{:S(2)}) async-start(bf16[8,32,1536]{2,1,0:T(8,128)(2,1)} %all_to_all.18), calls=%async_computation | async-start | bytes 1572864 | tf_op jit(solution)/shard_map/while/body/eval_jaxpr/all_to_all | solution.py:80
  211.3 4.3 %collective-permute-start.2 = (bf16[256,1536]{1,0:T(8,128)(2,1)}, bf16[256,1536]{1,0:T(8,128)(2,1)S(1)}, u32[]{:S(2)}, u32[]{:S(2)}) collective-permute-start(bf16[256,1536]{1,0:T(8,128)(2,1)} %fusion.52), channel_id=1, source_target_pairs={{0,8},{8,16},{16,24},{1,9},{9,17},{17,25},{2,10},{10,18},{18,26},{... | collective-permute-start | bytes 2359304 | tf_op jit(solution)/shard_map/while/body/eval_jaxpr/ppermute | solution.py:25
  215.7 8.3 %all-to-all-done = bf16[8,32,1536]{2,1,0:T(8,128)(2,1)S(1)} async-done(((bf16[8,32,1536]{2,1,0:T(8,128)(2,1)}), bf16[8,32,1536]{2,1,0:T(8,128)(2,1)S(1)}, u32[]{:S(2)}, u32[]{:S(2)}) %all-to-all-start) | async-done | bytes 786464 | tf_op jit(solution)/shard_map/while/body/eval_jaxpr/all_to_all | solution.py:80
  224.0 2.2 fusion.54
  226.1 7.2 %collective-permute-done.2 = bf16[256,1536]{1,0:T(8,128)(2,1)S(1)} collective-permute-done((bf16[256,1536]{1,0:T(8,128)(2,1)}, bf16[256,1536]{1,0:T(8,128)(2,1)S(1)}, u32[]{:S(2)}, u32[]{:S(2)}) %collective-permute-start.2) | collective-permute-done | bytes 786464 | tf_op jit(solution)/shard_map/while/body/eval_jaxpr/ppermute | solution.py:25
  233.4 1.5 fusion.49
  236.5 3.0 collective-permute-start.1
  240.3 5.4 %fusion.52 = bf16[256,1536]{1,0:T(8,128)(2,1)} fusion(bf16[256,1536]{1,0:T(8,128)(2,1)S(1)} %get-tuple-element.323, bf16[1536,1536]{1,0:T(8,128)(2,1)} %get-tuple-element.369, bf16[256,1536]{1,0:T(8,128)(2,1)S(1)} %fusion.50, bf16[2,1536]{1,0:T(2,128)(2,1)S(1)} %collective-permute-done, bf16[2,1536]{1,0:T(2,128)(2,1)S(1)} %collective-permute-done.1, ...), kind=kOutput, calls=%fused_computation.10.clone.1 | convolution fusion | flops 1222901760 | bytes 7120896 | tf_op jit(solution)/shard_map/while/body/eval_jaxpr/dot_general | solution.py:39
  248.8 5.9 %all-to-all-start = ((bf16[8,32,1536]{2,1,0:T(8,128)(2,1)}), bf16[8,32,1536]{2,1,0:T(8,128)(2,1)S(1)}, u32[]{:S(2)}, u32[]{:S(2)}) async-start(bf16[8,32,1536]{2,1,0:T(8,128)(2,1)} %all_to_all.18), calls=%async_computation | async-start | bytes 1572864 | tf_op jit(solution)/shard_map/while/body/eval_jaxpr/all_to_all | solution.py:80
  254.8 4.3 %collective-permute-start.2 = (bf16[256,1536]{1,0:T(8,128)(2,1)}, bf16[256,1536]{1,0:T(8,128)(2,1)S(1)}, u32[]{:S(2)}, u32[]{:S(2)}) collective-permute-start(bf16[256,1536]{1,0:T(8,128)(2,1)} %fusion.52), channel_id=1, source_target_pairs={{0,8},{8,16},{16,24},{1,9},{9,17},{17,25},{2,10},{10,18},{18,26},{... | collective-permute-start | bytes 2359304 | tf_op jit(solution)/shard_map/while/body/eval_jaxpr/ppermute | solution.py:25
  259.1 8.3 %all-to-all-done = bf16[8,32,1536]{2,1,0:T(8,128)(2,1)S(1)} async-done(((bf16[8,32,1536]{2,1,0:T(8,128)(2,1)}), bf16[8,32,1536]{2,1,0:T(8,128)(2,1)S(1)}, u32[]{:S(2)}, u32[]{:S(2)}) %all-to-all-start) | async-done | bytes 786464 | tf_op jit(solution)/shard_map/while/body/eval_jaxpr/all_to_all | solution.py:80
  267.4 2.2 fusion.54
  269.6 7.2 %collective-permute-done.2 = bf16[256,1536]{1,0:T(8,128)(2,1)S(1)} collective-permute-done((bf16[256,1536]{1,0:T(8,128)(2,1)}, bf16[256,1536]{1,0:T(8,128)(2,1)S(1)}, u32[]{:S(2)}, u32[]{:S(2)}) %collective-permute-start.2) | collective-permute-done | bytes 786464 | tf_op jit(solution)/shard_map/while/body/eval_jaxpr/ppermute | solution.py:25
  276.8 1.5 fusion.49
  279.9 3.0 collective-permute-start.1
  283.8 5.4 %fusion.52 = bf16[256,1536]{1,0:T(8,128)(2,1)} fusion(bf16[256,1536]{1,0:T(8,128)(2,1)S(1)} %get-tuple-element.323, bf16[1536,1536]{1,0:T(8,128)(2,1)} %get-tuple-element.369, bf16[256,1536]{1,0:T(8,128)(2,1)S(1)} %fusion.50, bf16[2,1536]{1,0:T(2,128)(2,1)S(1)} %collective-permute-done, bf16[2,1536]{1,0:T(2,128)(2,1)S(1)} %collective-permute-done.1, ...), kind=kOutput, calls=%fused_computation.10.clone.1 | convolution fusion | flops 1222901760 | bytes 7120896 | tf_op jit(solution)/shard_map/while/body/eval_jaxpr/dot_general | solution.py:39
  292.2 5.9 %all-to-all-start = ((bf16[8,32,1536]{2,1,0:T(8,128)(2,1)}), bf16[8,32,1536]{2,1,0:T(8,128)(2,1)S(1)}, u32[]{:S(2)}, u32[]{:S(2)}) async-start(bf16[8,32,1536]{2,1,0:T(8,128)(2,1)} %all_to_all.18), calls=%async_computation | async-start | bytes 1572864 | tf_op jit(solution)/shard_map/while/body/eval_jaxpr/all_to_all | solution.py:80
  298.2 4.3 %collective-permute-start.2 = (bf16[256,1536]{1,0:T(8,128)(2,1)}, bf16[256,1536]{1,0:T(8,128)(2,1)S(1)}, u32[]{:S(2)}, u32[]{:S(2)}) collective-permute-start(bf16[256,1536]{1,0:T(8,128)(2,1)} %fusion.52), channel_id=1, source_target_pairs={{0,8},{8,16},{16,24},{1,9},{9,17},{17,25},{2,10},{10,18},{18,26},{... | collective-permute-start | bytes 2359304 | tf_op jit(solution)/shard_map/while/body/eval_jaxpr/ppermute | solution.py:25
  302.5 8.3 %all-to-all-done = bf16[8,32,1536]{2,1,0:T(8,128)(2,1)S(1)} async-done(((bf16[8,32,1536]{2,1,0:T(8,128)(2,1)}), bf16[8,32,1536]{2,1,0:T(8,128)(2,1)S(1)}, u32[]{:S(2)}, u32[]{:S(2)}) %all-to-all-start) | async-done | bytes 786464 | tf_op jit(solution)/shard_map/while/body/eval_jaxpr/all_to_all | solution.py:80
  310.8 2.2 fusion.54
  313.0 7.2 %collective-permute-done.2 = bf16[256,1536]{1,0:T(8,128)(2,1)S(1)} collective-permute-done((bf16[256,1536]{1,0:T(8,128)(2,1)}, bf16[256,1536]{1,0:T(8,128)(2,1)S(1)}, u32[]{:S(2)}, u32[]{:S(2)}) %collective-permute-start.2) | collective-permute-done | bytes 786464 | tf_op jit(solution)/shard_map/while/body/eval_jaxpr/ppermute | solution.py:25
  (85 shorter events, 36.9 us)
Async XLA Ops:
  0.0 8.2 %copy-start = (bf16[512,1536]{1,0:T(8,128)(2,1)S(1)}, bf16[512,1536]{1,0:T(8,128)(2,1)}, u32[]{:S(2)}) copy-start(bf16[512,1536]{1,0:T(8,128)(2,1)} %param.9) | copy-start | bytes 4718596
  13.4 1.9 copy-start.1
  17.1 4.4 %collective-permute-start = (bf16[2,1536]{1,0:T(2,128)(2,1)S(1)}, bf16[2,1536]{1,0:T(2,128)(2,1)S(1)}, u32[]{:S(2)}, u32[]{:S(2)}) collective-permute-start(bf16[2,1536]{1,0:T(2,128)(2,1)S(1)} %get-tuple-element.325), channel_id=1, source_target_pairs={{1,0},{2,1},{3,2},{4,3},{5,4},{6,5},{7,6},{9,8},{10,9},{11,10},{12... | collective-permute-start | bytes 18440 | tf_op jit(solution)/shard_map/while/body/eval_jaxpr/ppermute | solution.py:17
  18.4 3.8 %collective-permute-start.1 = (bf16[2,1536]{1,0:T(2,128)(2,1)S(1)}, bf16[2,1536]{1,0:T(2,128)(2,1)S(1)}, u32[]{:S(2)}, u32[]{:S(2)}) collective-permute-start(bf16[2,1536]{1,0:T(2,128)(2,1)S(1)} %get-tuple-element.326), channel_id=1, source_target_pairs={{0,1},{1,2},{2,3},{3,4},{4,5},{5,6},{6,7},{8,9},{9,10},{10,11},{11... | collective-permute-start | bytes 18440 | tf_op jit(solution)/shard_map/while/body/eval_jaxpr/ppermute | solution.py:14
  30.7 20.3 %all-to-all-start = ((bf16[8,32,1536]{2,1,0:T(8,128)(2,1)}), bf16[8,32,1536]{2,1,0:T(8,128)(2,1)S(1)}, u32[]{:S(2)}, u32[]{:S(2)}) async-start(bf16[8,32,1536]{2,1,0:T(8,128)(2,1)} %all_to_all.18), calls=%async_computation | async-start | bytes 1572864 | tf_op jit(solution)/shard_map/while/body/eval_jaxpr/all_to_all | solution.py:80
  38.5 21.2 %collective-permute-start.2 = (bf16[256,1536]{1,0:T(8,128)(2,1)}, bf16[256,1536]{1,0:T(8,128)(2,1)S(1)}, u32[]{:S(2)}, u32[]{:S(2)}) collective-permute-start(bf16[256,1536]{1,0:T(8,128)(2,1)} %fusion.52), channel_id=1, source_target_pairs={{0,8},{8,16},{16,24},{1,9},{9,17},{17,25},{2,10},{10,18},{18,26},{... | collective-permute-start | bytes 2359304 | tf_op jit(solution)/shard_map/while/body/eval_jaxpr/ppermute | solution.py:25
  61.5 4.4 %collective-permute-start = (bf16[2,1536]{1,0:T(2,128)(2,1)S(1)}, bf16[2,1536]{1,0:T(2,128)(2,1)S(1)}, u32[]{:S(2)}, u32[]{:S(2)}) collective-permute-start(bf16[2,1536]{1,0:T(2,128)(2,1)S(1)} %get-tuple-element.325), channel_id=1, source_target_pairs={{1,0},{2,1},{3,2},{4,3},{5,4},{6,5},{7,6},{9,8},{10,9},{11,10},{12... | collective-permute-start | bytes 18440 | tf_op jit(solution)/shard_map/while/body/eval_jaxpr/ppermute | solution.py:17
  62.8 3.8 %collective-permute-start.1 = (bf16[2,1536]{1,0:T(2,128)(2,1)S(1)}, bf16[2,1536]{1,0:T(2,128)(2,1)S(1)}, u32[]{:S(2)}, u32[]{:S(2)}) collective-permute-start(bf16[2,1536]{1,0:T(2,128)(2,1)S(1)} %get-tuple-element.326), channel_id=1, source_target_pairs={{0,1},{1,2},{2,3},{3,4},{4,5},{5,6},{6,7},{8,9},{9,10},{10,11},{11... | collective-permute-start | bytes 18440 | tf_op jit(solution)/shard_map/while/body/eval_jaxpr/ppermute | solution.py:14
  75.1 18.6 %all-to-all-start = ((bf16[8,32,1536]{2,1,0:T(8,128)(2,1)}), bf16[8,32,1536]{2,1,0:T(8,128)(2,1)S(1)}, u32[]{:S(2)}, u32[]{:S(2)}) async-start(bf16[8,32,1536]{2,1,0:T(8,128)(2,1)} %all_to_all.18), calls=%async_computation | async-start | bytes 1572864 | tf_op jit(solution)/shard_map/while/body/eval_jaxpr/all_to_all | solution.py:80
  81.1 22.0 %collective-permute-start.2 = (bf16[256,1536]{1,0:T(8,128)(2,1)}, bf16[256,1536]{1,0:T(8,128)(2,1)S(1)}, u32[]{:S(2)}, u32[]{:S(2)}) collective-permute-start(bf16[256,1536]{1,0:T(8,128)(2,1)} %fusion.52), channel_id=1, source_target_pairs={{0,8},{8,16},{16,24},{1,9},{9,17},{17,25},{2,10},{10,18},{18,26},{... | collective-permute-start | bytes 2359304 | tf_op jit(solution)/shard_map/while/body/eval_jaxpr/ppermute | solution.py:25
  104.9 4.4 %collective-permute-start = (bf16[2,1536]{1,0:T(2,128)(2,1)S(1)}, bf16[2,1536]{1,0:T(2,128)(2,1)S(1)}, u32[]{:S(2)}, u32[]{:S(2)}) collective-permute-start(bf16[2,1536]{1,0:T(2,128)(2,1)S(1)} %get-tuple-element.325), channel_id=1, source_target_pairs={{1,0},{2,1},{3,2},{4,3},{5,4},{6,5},{7,6},{9,8},{10,9},{11,10},{12... | collective-permute-start | bytes 18440 | tf_op jit(solution)/shard_map/while/body/eval_jaxpr/ppermute | solution.py:17
  106.2 3.8 %collective-permute-start.1 = (bf16[2,1536]{1,0:T(2,128)(2,1)S(1)}, bf16[2,1536]{1,0:T(2,128)(2,1)S(1)}, u32[]{:S(2)}, u32[]{:S(2)}) collective-permute-start(bf16[2,1536]{1,0:T(2,128)(2,1)S(1)} %get-tuple-element.326), channel_id=1, source_target_pairs={{0,1},{1,2},{2,3},{3,4},{4,5},{5,6},{6,7},{8,9},{9,10},{10,11},{11... | collective-permute-start | bytes 18440 | tf_op jit(solution)/shard_map/while/body/eval_jaxpr/ppermute | solution.py:14
  118.6 18.6 %all-to-all-start = ((bf16[8,32,1536]{2,1,0:T(8,128)(2,1)}), bf16[8,32,1536]{2,1,0:T(8,128)(2,1)S(1)}, u32[]{:S(2)}, u32[]{:S(2)}) async-start(bf16[8,32,1536]{2,1,0:T(8,128)(2,1)} %all_to_all.18), calls=%async_computation | async-start | bytes 1572864 | tf_op jit(solution)/shard_map/while/body/eval_jaxpr/all_to_all | solution.py:80
  124.5 22.0 %collective-permute-start.2 = (bf16[256,1536]{1,0:T(8,128)(2,1)}, bf16[256,1536]{1,0:T(8,128)(2,1)S(1)}, u32[]{:S(2)}, u32[]{:S(2)}) collective-permute-start(bf16[256,1536]{1,0:T(8,128)(2,1)} %fusion.52), channel_id=1, source_target_pairs={{0,8},{8,16},{16,24},{1,9},{9,17},{17,25},{2,10},{10,18},{18,26},{... | collective-permute-start | bytes 2359304 | tf_op jit(solution)/shard_map/while/body/eval_jaxpr/ppermute | solution.py:25
  148.4 4.4 %collective-permute-start = (bf16[2,1536]{1,0:T(2,128)(2,1)S(1)}, bf16[2,1536]{1,0:T(2,128)(2,1)S(1)}, u32[]{:S(2)}, u32[]{:S(2)}) collective-permute-start(bf16[2,1536]{1,0:T(2,128)(2,1)S(1)} %get-tuple-element.325), channel_id=1, source_target_pairs={{1,0},{2,1},{3,2},{4,3},{5,4},{6,5},{7,6},{9,8},{10,9},{11,10},{12... | collective-permute-start | bytes 18440 | tf_op jit(solution)/shard_map/while/body/eval_jaxpr/ppermute | solution.py:17
  149.7 3.8 %collective-permute-start.1 = (bf16[2,1536]{1,0:T(2,128)(2,1)S(1)}, bf16[2,1536]{1,0:T(2,128)(2,1)S(1)}, u32[]{:S(2)}, u32[]{:S(2)}) collective-permute-start(bf16[2,1536]{1,0:T(2,128)(2,1)S(1)} %get-tuple-element.326), channel_id=1, source_target_pairs={{0,1},{1,2},{2,3},{3,4},{4,5},{5,6},{6,7},{8,9},{9,10},{10,11},{11... | collective-permute-start | bytes 18440 | tf_op jit(solution)/shard_map/while/body/eval_jaxpr/ppermute | solution.py:14
  162.0 18.6 %all-to-all-start = ((bf16[8,32,1536]{2,1,0:T(8,128)(2,1)}), bf16[8,32,1536]{2,1,0:T(8,128)(2,1)S(1)}, u32[]{:S(2)}, u32[]{:S(2)}) async-start(bf16[8,32,1536]{2,1,0:T(8,128)(2,1)} %all_to_all.18), calls=%async_computation | async-start | bytes 1572864 | tf_op jit(solution)/shard_map/while/body/eval_jaxpr/all_to_all | solution.py:80
  167.9 22.0 %collective-permute-start.2 = (bf16[256,1536]{1,0:T(8,128)(2,1)}, bf16[256,1536]{1,0:T(8,128)(2,1)S(1)}, u32[]{:S(2)}, u32[]{:S(2)}) collective-permute-start(bf16[256,1536]{1,0:T(8,128)(2,1)} %fusion.52), channel_id=1, source_target_pairs={{0,8},{8,16},{16,24},{1,9},{9,17},{17,25},{2,10},{10,18},{18,26},{... | collective-permute-start | bytes 2359304 | tf_op jit(solution)/shard_map/while/body/eval_jaxpr/ppermute | solution.py:25
  191.8 4.4 %collective-permute-start = (bf16[2,1536]{1,0:T(2,128)(2,1)S(1)}, bf16[2,1536]{1,0:T(2,128)(2,1)S(1)}, u32[]{:S(2)}, u32[]{:S(2)}) collective-permute-start(bf16[2,1536]{1,0:T(2,128)(2,1)S(1)} %get-tuple-element.325), channel_id=1, source_target_pairs={{1,0},{2,1},{3,2},{4,3},{5,4},{6,5},{7,6},{9,8},{10,9},{11,10},{12... | collective-permute-start | bytes 18440 | tf_op jit(solution)/shard_map/while/body/eval_jaxpr/ppermute | solution.py:17
  193.1 3.8 %collective-permute-start.1 = (bf16[2,1536]{1,0:T(2,128)(2,1)S(1)}, bf16[2,1536]{1,0:T(2,128)(2,1)S(1)}, u32[]{:S(2)}, u32[]{:S(2)}) collective-permute-start(bf16[2,1536]{1,0:T(2,128)(2,1)S(1)} %get-tuple-element.326), channel_id=1, source_target_pairs={{0,1},{1,2},{2,3},{3,4},{4,5},{5,6},{6,7},{8,9},{9,10},{10,11},{11... | collective-permute-start | bytes 18440 | tf_op jit(solution)/shard_map/while/body/eval_jaxpr/ppermute | solution.py:14
  205.4 18.6 %all-to-all-start = ((bf16[8,32,1536]{2,1,0:T(8,128)(2,1)}), bf16[8,32,1536]{2,1,0:T(8,128)(2,1)S(1)}, u32[]{:S(2)}, u32[]{:S(2)}) async-start(bf16[8,32,1536]{2,1,0:T(8,128)(2,1)} %all_to_all.18), calls=%async_computation | async-start | bytes 1572864 | tf_op jit(solution)/shard_map/while/body/eval_jaxpr/all_to_all | solution.py:80
  211.3 22.0 %collective-permute-start.2 = (bf16[256,1536]{1,0:T(8,128)(2,1)}, bf16[256,1536]{1,0:T(8,128)(2,1)S(1)}, u32[]{:S(2)}, u32[]{:S(2)}) collective-permute-start(bf16[256,1536]{1,0:T(8,128)(2,1)} %fusion.52), channel_id=1, source_target_pairs={{0,8},{8,16},{16,24},{1,9},{9,17},{17,25},{2,10},{10,18},{18,26},{... | collective-permute-start | bytes 2359304 | tf_op jit(solution)/shard_map/while/body/eval_jaxpr/ppermute | solution.py:25
  235.2 4.4 %collective-permute-start = (bf16[2,1536]{1,0:T(2,128)(2,1)S(1)}, bf16[2,1536]{1,0:T(2,128)(2,1)S(1)}, u32[]{:S(2)}, u32[]{:S(2)}) collective-permute-start(bf16[2,1536]{1,0:T(2,128)(2,1)S(1)} %get-tuple-element.325), channel_id=1, source_target_pairs={{1,0},{2,1},{3,2},{4,3},{5,4},{6,5},{7,6},{9,8},{10,9},{11,10},{12... | collective-permute-start | bytes 18440 | tf_op jit(solution)/shard_map/while/body/eval_jaxpr/ppermute | solution.py:17
  236.5 3.8 %collective-permute-start.1 = (bf16[2,1536]{1,0:T(2,128)(2,1)S(1)}, bf16[2,1536]{1,0:T(2,128)(2,1)S(1)}, u32[]{:S(2)}, u32[]{:S(2)}) collective-permute-start(bf16[2,1536]{1,0:T(2,128)(2,1)S(1)} %get-tuple-element.326), channel_id=1, source_target_pairs={{0,1},{1,2},{2,3},{3,4},{4,5},{5,6},{6,7},{8,9},{9,10},{10,11},{11... | collective-permute-start | bytes 18440 | tf_op jit(solution)/shard_map/while/body/eval_jaxpr/ppermute | solution.py:14
  248.8 18.6 %all-to-all-start = ((bf16[8,32,1536]{2,1,0:T(8,128)(2,1)}), bf16[8,32,1536]{2,1,0:T(8,128)(2,1)S(1)}, u32[]{:S(2)}, u32[]{:S(2)}) async-start(bf16[8,32,1536]{2,1,0:T(8,128)(2,1)} %all_to_all.18), calls=%async_computation | async-start | bytes 1572864 | tf_op jit(solution)/shard_map/while/body/eval_jaxpr/all_to_all | solution.py:80
  254.8 22.0 %collective-permute-start.2 = (bf16[256,1536]{1,0:T(8,128)(2,1)}, bf16[256,1536]{1,0:T(8,128)(2,1)S(1)}, u32[]{:S(2)}, u32[]{:S(2)}) collective-permute-start(bf16[256,1536]{1,0:T(8,128)(2,1)} %fusion.52), channel_id=1, source_target_pairs={{0,8},{8,16},{16,24},{1,9},{9,17},{17,25},{2,10},{10,18},{18,26},{... | collective-permute-start | bytes 2359304 | tf_op jit(solution)/shard_map/while/body/eval_jaxpr/ppermute | solution.py:25
  278.6 4.4 %collective-permute-start = (bf16[2,1536]{1,0:T(2,128)(2,1)S(1)}, bf16[2,1536]{1,0:T(2,128)(2,1)S(1)}, u32[]{:S(2)}, u32[]{:S(2)}) collective-permute-start(bf16[2,1536]{1,0:T(2,128)(2,1)S(1)} %get-tuple-element.325), channel_id=1, source_target_pairs={{1,0},{2,1},{3,2},{4,3},{5,4},{6,5},{7,6},{9,8},{10,9},{11,10},{12... | collective-permute-start | bytes 18440 | tf_op jit(solution)/shard_map/while/body/eval_jaxpr/ppermute | solution.py:17
  279.9 3.8 %collective-permute-start.1 = (bf16[2,1536]{1,0:T(2,128)(2,1)S(1)}, bf16[2,1536]{1,0:T(2,128)(2,1)S(1)}, u32[]{:S(2)}, u32[]{:S(2)}) collective-permute-start(bf16[2,1536]{1,0:T(2,128)(2,1)S(1)} %get-tuple-element.326), channel_id=1, source_target_pairs={{0,1},{1,2},{2,3},{3,4},{4,5},{5,6},{6,7},{8,9},{9,10},{10,11},{11... | collective-permute-start | bytes 18440 | tf_op jit(solution)/shard_map/while/body/eval_jaxpr/ppermute | solution.py:14
  292.2 18.6 %all-to-all-start = ((bf16[8,32,1536]{2,1,0:T(8,128)(2,1)}), bf16[8,32,1536]{2,1,0:T(8,128)(2,1)S(1)}, u32[]{:S(2)}, u32[]{:S(2)}) async-start(bf16[8,32,1536]{2,1,0:T(8,128)(2,1)} %all_to_all.18), calls=%async_computation | async-start | bytes 1572864 | tf_op jit(solution)/shard_map/while/body/eval_jaxpr/all_to_all | solution.py:80
  298.2 22.0 %collective-permute-start.2 = (bf16[256,1536]{1,0:T(8,128)(2,1)}, bf16[256,1536]{1,0:T(8,128)(2,1)S(1)}, u32[]{:S(2)}, u32[]{:S(2)}) collective-permute-start(bf16[256,1536]{1,0:T(8,128)(2,1)} %fusion.52), channel_id=1, source_target_pairs={{0,8},{8,16},{16,24},{1,9},{9,17},{17,25},{2,10},{10,18},{18,26},{... | collective-permute-start | bytes 2359304 | tf_op jit(solution)/shard_map/while/body/eval_jaxpr/ppermute | solution.py:25
where the time goes:
time: 322 us; the launch traced here: 320 us
  waiting for transfers between devices  114 us (35%)
  starting transfers between devices  103 us (32%)
  matrix products  45.4 us (14%)
  local copies, waits for them, and re-layouts  29 us (9%)
  other arithmetic  28.6 us (9%)
    all_to_all x7, waiting for transfers between devices, advance(): lax.all_to_all(arrange(leaving), 'seq', split_axis=0, concat_axis=0, tile...  58.7 us
    ppermute x7, waiting for transfers between devices, passed_along(): lax.ppermute(value, axis, [(source, source + steps) for source in range(i...  49.9 us
    all_to_all x7, starting transfers between devices, advance(): lax.all_to_all(arrange(leaving), 'seq', split_axis=0, concat_axis=0, tile...  43.4 us
    dot_general x7, matrix products, section_block(): update = jnp.dot(mixed, weight, preferred_element_type=jnp.float32)  37.8 us
    ppermute x7, starting transfers between devices, passed_along(): lax.ppermute(value, axis, [(source, source + steps) for source in range(i...  29.4 us
    ppermute x7, starting transfers between devices, extended(): lax.ppermute(lax.slice_in_dim(block, block.shape[dim] - width, None, axis...  21.2 us
    dynamic_update_slice x7, other arithmetic, advance(): hint_rows = lax.dynamic_update_index_in_dim(hint_rows, arrived, slot_idx, 0)  15.4 us
    reduce_sum x7, other arithmetic, section_block(): jnp.mean(wide_state * wide_state, axis=-1, keepdims=True) + 1e-06  10.4 us
  transfers between devices with their start and end apart: 28, of which 21 were waited for; matrix products, arithmetic and copies ran while one was open for 5% of the time, Pallas kernels for 0%

commit v1 on v0

--- a/solution.py
+++ b/solution.py
@@ -2,8 +2,28 @@
 import jax.numpy as jnp
 from jax import lax
 from jax.sharding import PartitionSpec as P
+from jax.lax import axis_index, axis_size, ppermute
 
 BLOCK_BP = 128
+
+
+def _connect_pages(state, at_axis, which_dim):
+    state_now = axis_size("seq")
+    later, new = (state_now, axis_index("seq"))
+    w_next = list(state.shape)
+    answer = state.shape[at_axis] // later
+    w_next[at_axis] = answer
+    local_next = w_next[which_dim]
+    w_next[which_dim] = local_next * later
+    raw_out = jnp.zeros(w_next, state.dtype)
+    for t in tuple(range(later)):
+        part_next = lax.dynamic_slice_in_dim(state, (new ^ t) * answer, answer, axis=at_axis)
+        if t:
+            part_next = ppermute(part_next, "seq", [(dev, dev ^ t) for dev in range(later)])
+        raw_out = lax.dynamic_update_slice_in_dim(
+            raw_out, part_next, (new ^ t) * local_next, axis=which_dim
+        )
+    return raw_out
 
 
 def extended(block, sides, width):
@@ -77,7 +97,7 @@
         micro_idx = moment - section_id
         slot_idx = jnp.clip(micro_idx, 0, micro_count - 1)
         in_range = (micro_idx >= 0) & (micro_idx < micro_count)
-        arrived = lax.all_to_all(arrange(leaving), "seq", split_axis=0, concat_axis=0, tiled=True)
+        arrived = _connect_pages(arrange(leaving), 0, 0)
         previous = lax.dynamic_index_in_dim(hint_rows, slot_idx, 0, keepdims=False)
         arrived = jnp.where(in_range, arrived, previous)
         hint_rows = lax.dynamic_update_index_in_dim(hint_rows, arrived, slot_idx, 0)

time: 322 us -> 311 us (0.966)
  waiting for transfers between devices: 114 us -> 31.6 us
  starting transfers between devices: 103 us -> 155 us
  local copies, waits for them, and re-layouts: 29 us -> 52.3 us
  other arithmetic: 28.6 us -> 20.7 us
    ppermute x0 -> x49, starting transfers between devices: none -> 87.1 us  [_connect_pages(): ppermute(part_next, 'seq', [(dev, dev ^ t) for dev in range(later)])]
    all_to_all x7 -> x0, waiting for transfers between devices: 58.7 us -> none  [advance(): lax.all_to_all(arrange(leaving), 'seq', split_axis=0, concat_axis=0, tile...]
    ppermute x7, waiting for transfers between devices: 49.9 us -> 0.42 us  [passed_along(): lax.ppermute(value, axis, [(source, source + steps) for source in range(i...]
    all_to_all x7 -> x0, starting transfers between devices: 43.4 us -> none  [advance(): lax.all_to_all(arrange(leaving), 'seq', split_axis=0, concat_axis=0, tile...]
    ppermute x0 -> x49, waiting for transfers between devices: none -> 31.1 us  [_connect_pages(): ppermute(part_next, 'seq', [(dev, dev ^ t) for dev in range(later)])]
    dynamic_slice x0 -> x14, local copies, waits for them, and re-layouts: none -> 13.6 us  [the longest x7 8.29 us: advance(): previous = lax.dynamic_index_in_dim(hint_rows, slot_idx, 0, keepdims=False)]
    all_to_all x7 -> x0, local copies, waits for them, and re-layouts: 8.67 us -> none  [advance(): lax.all_to_all(arrange(leaving), 'seq', split_axis=0, concat_axis=0, tile...]
    ppermute x7, starting transfers between devices: 29.4 us -> 37.7 us  [passed_along(): lax.ppermute(value, axis, [(source, source + steps) for source in range(i...]
  transfers between devices with their start and end apart: 28 -> 70, of which waited for: 21 -> 8; matrix products, arithmetic and copies ran while one was open for 5% -> 10% of each run, Pallas kernels for 0% -> 0%
where the time goes in v1:
time: 311 us; the launch traced here: 307 us
  starting transfers between devices  155 us (50%)
  local copies, waits for them, and re-layouts  52.3 us (17%)
  matrix products  45.4 us (15%)
  waiting for transfers between devices  31.6 us (10%)
  other arithmetic  20.7 us (7%)
    ppermute x49, starting transfers between devices, _connect_pages(): ppermute(part_next, 'seq', [(dev, dev ^ t) for dev in range(later)])  87.1 us
    dot_general x7, matrix products, section_block(): update = jnp.dot(mixed, weight, preferred_element_type=jnp.float32)  37.8 us
    ppermute x7, starting transfers between devices, passed_along(): lax.ppermute(value, axis, [(source, source + steps) for source in range(i...  37.7 us
    ppermute x49, waiting for transfers between devices, _connect_pages(): ppermute(part_next, 'seq', [(dev, dev ^ t) for dev in range(later)])  31.1 us
    ppermute x7, starting transfers between devices, extended(): lax.ppermute(lax.slice_in_dim(block, block.shape[dim] - width, None, axis...  21.2 us
    reduce_sum x7, other arithmetic, section_block(): jnp.mean(wide_state * wide_state, axis=-1, keepdims=True) + 1e-06  10.5 us
    reshape x7, local copies, waits for them, and re-layouts, arrange(): grouped = current.reshape(segs_dev, seg_rows * channels)  10.3 us
    ppermute x7, starting transfers between devices, extended(): lax.ppermute(lax.slice_in_dim(block, 0, width, axis=dim), axis, backward)  9.04 us
  transfers between devices with their start and end apart: 70, of which 8 were waited for; matrix products, arithmetic and copies ran while one was open for 10% of the time, Pallas kernels for 0%

profile of v1, /device:TPU:0, one launch (start us, length us, event | category | flops | bytes accessed | tf_op | source)
XLA Modules:
  0.0 306.6 jit_solution(3524165156307571791)
XLA Ops:
  3.9 1.9 eq.49
  5.8 3.0 eq.50
  8.8 5.2 %convolution_convert_fusion.1 = bf16[1024,1536]{1,0:T(8,128)(2,1)} fusion(bf16[512,1536]{1,0:T(8,128)(2,1)S(1)} %copy-done, s32[1024,512]{0,1:T(8,128)} %eq.50, s32[512]{0:T(512)S(1)} %eq.52), kind=kOutput, calls=%fused_computation.64 | convolution fusion | flops 1612709888 | bytes 6817792 | tf_op jit(solution)/shard_map/dot_general | solution.py:75
  14.9 1.9 broadcast_in_dim.21
  16.8 289.8 %while.17 = (s32[]{:T(128)}, bf16[256,1536]{1,0:T(8,128)(2,1)}, bf16[4,256,1536]{2,1,0:T(8,128)(2,1)}, pred[]{:T(512)}, bf16[4,256,1536]{2,1,0:T(8,128)(2,1)}, /...) while((s32[]{:T(128)}, bf16[256,1536]{1,0:T(8,128)(2,1)}, ...), condition=%wide.region_2.3_spmd.clone, body=%wide.region_0.2_spmd.clone.sunk | while | flops 1252002048 | bytes 29496644 | solution.py:109
  19.9 3.0 collective-permute-start.1
  24.1 5.4 %fusion.50 = bf16[256,1536]{1,0:T(8,128)(2,1)} fusion(bf16[256,1536]{1,0:T(8,128)(2,1)S(1)} %get-tuple-element.339, bf16[1536,1536]{1,0:T(8,128)(2,1)} %get-tuple-element.409, bf16[256,1536]{1,0:T(8,128)(2,1)S(1)} %fusion.48, bf16[2,1536]{1,0:T(2,128)(2,1)S(1)} %collective-permute-done, bf16[2,1536]{1,0:T(2,128)(2,1)S(1)} %collective-permute-done.1, ...), kind=kOutput, calls=%fused_computation.10.clone.1 | convolution fusion | flops 1222901760 | bytes 7120896 | tf_op jit(solution)/shard_map/while/body/eval_jaxpr/dot_general | solution.py:59
  32.5 2.5 collective-permute-start.3
  36.3 4.6 %collective-permute-start.2 = (bf16[256,1536]{1,0:T(8,128)(2,1)}, bf16[256,1536]{1,0:T(8,128)(2,1)}, u32[]{:S(2)}, u32[]{:S(2)}) collective-permute-start(bf16[256,1536]{1,0:T(8,128)(2,1)} %fusion.50), channel_id=1, source_target_pairs={{0,8},{8,16},{16,24},{1,9},{9,17},{17,25},{2,10},{10,18},{18,26},{... | collective-permute-start | bytes 2359304 | tf_op jit(solution)/shard_map/while/body/eval_jaxpr/ppermute | solution.py:45
  40.9 2.4 collective-permute-start.4
  43.3 2.7 collective-permute-start.6
  47.1 2.3 collective-permute-start.8
  49.5 1.7 collective-permute-start.9
  51.2 4.6 %collective-permute-done.7 = bf16[32,1536]{1,0:T(8,128)(2,1)S(1)} collective-permute-done((bf16[32,1536]{1,0:T(8,128)(2,1)S(1)}, bf16[32,1536]{1,0:T(8,128)(2,1)S(1)}, u32[]{:S(2)}, u32[]{:S(2)}) %collective-permute-start.7) | collective-permute-done | bytes 98336 | tf_op jit(solution)/shard_map/while/body/eval_jaxpr/ppermute | solution.py:22
  60.4 3.0 collective-permute-start.1
  64.6 5.4 %fusion.50 = bf16[256,1536]{1,0:T(8,128)(2,1)} fusion(bf16[256,1536]{1,0:T(8,128)(2,1)S(1)} %get-tuple-element.339, bf16[1536,1536]{1,0:T(8,128)(2,1)} %get-tuple-element.409, bf16[256,1536]{1,0:T(8,128)(2,1)S(1)} %fusion.48, bf16[2,1536]{1,0:T(2,128)(2,1)S(1)} %collective-permute-done, bf16[2,1536]{1,0:T(2,128)(2,1)S(1)} %collective-permute-done.1, ...), kind=kOutput, calls=%fused_computation.10.clone.1 | convolution fusion | flops 1222901760 | bytes 7120896 | tf_op jit(solution)/shard_map/while/body/eval_jaxpr/dot_general | solution.py:59
  73.0 2.0 collective-permute-start.3
  76.2 5.5 %collective-permute-start.2 = (bf16[256,1536]{1,0:T(8,128)(2,1)}, bf16[256,1536]{1,0:T(8,128)(2,1)}, u32[]{:S(2)}, u32[]{:S(2)}) collective-permute-start(bf16[256,1536]{1,0:T(8,128)(2,1)} %fusion.50), channel_id=1, source_target_pairs={{0,8},{8,16},{16,24},{1,9},{9,17},{17,25},{2,10},{10,18},{18,26},{... | collective-permute-start | bytes 2359304 | tf_op jit(solution)/shard_map/while/body/eval_jaxpr/ppermute | solution.py:45
  81.7 3.1 %collective-permute-start.4 = (bf16[32,1536]{1,0:T(8,128)(2,1)}, bf16[32,1536]{1,0:T(8,128)(2,1)S(1)}, u32[]{:S(2)}, u32[]{:S(2)}) collective-permute-start(bf16[32,1536]{1,0:T(8,128)(2,1)} %get-tuple-element.350), channel_id=1, source_target_pairs={{0,2},{1,3},{2,0},{3,1},{4,6},{5,7},{6,4},{7,5},{8,10},{9,11},{10,... | collective-permute-start | bytes 294920 | tf_op jit(solution)/shard_map/while/body/eval_jaxpr/ppermute | solution.py:22
  84.9 2.7 collective-permute-start.6
  88.8 2.6 collective-permute-start.8
  91.4 1.5 collective-permute-start.9
  93.0 4.4 %collective-permute-done.7 = bf16[32,1536]{1,0:T(8,128)(2,1)S(1)} collective-permute-done((bf16[32,1536]{1,0:T(8,128)(2,1)S(1)}, bf16[32,1536]{1,0:T(8,128)(2,1)S(1)}, u32[]{:S(2)}, u32[]{:S(2)}) %collective-permute-start.7) | collective-permute-done | bytes 98336 | tf_op jit(solution)/shard_map/while/body/eval_jaxpr/ppermute | solution.py:22
  101.6 3.0 collective-permute-start.1
  105.9 5.4 %fusion.50 = bf16[256,1536]{1,0:T(8,128)(2,1)} fusion(bf16[256,1536]{1,0:T(8,128)(2,1)S(1)} %get-tuple-element.339, bf16[1536,1536]{1,0:T(8,128)(2,1)} %get-tuple-element.409, bf16[256,1536]{1,0:T(8,128)(2,1)S(1)} %fusion.48, bf16[2,1536]{1,0:T(2,128)(2,1)S(1)} %collective-permute-done, bf16[2,1536]{1,0:T(2,128)(2,1)S(1)} %collective-permute-done.1, ...), kind=kOutput, calls=%fused_computation.10.clone.1 | convolution fusion | flops 1222901760 | bytes 7120896 | tf_op jit(solution)/shard_map/while/body/eval_jaxpr/dot_general | solution.py:59
  114.3 2.4 collective-permute-start.3
  117.8 5.5 %collective-permute-start.2 = (bf16[256,1536]{1,0:T(8,128)(2,1)}, bf16[256,1536]{1,0:T(8,128)(2,1)}, u32[]{:S(2)}, u32[]{:S(2)}) collective-permute-start(bf16[256,1536]{1,0:T(8,128)(2,1)} %fusion.50), channel_id=1, source_target_pairs={{0,8},{8,16},{16,24},{1,9},{9,17},{17,25},{2,10},{10,18},{18,26},{... | collective-permute-start | bytes 2359304 | tf_op jit(solution)/shard_map/while/body/eval_jaxpr/ppermute | solution.py:45
  123.4 3.1 %collective-permute-start.4 = (bf16[32,1536]{1,0:T(8,128)(2,1)}, bf16[32,1536]{1,0:T(8,128)(2,1)S(1)}, u32[]{:S(2)}, u32[]{:S(2)}) collective-permute-start(bf16[32,1536]{1,0:T(8,128)(2,1)} %get-tuple-element.350), channel_id=1, source_target_pairs={{0,2},{1,3},{2,0},{3,1},{4,6},{5,7},{6,4},{7,5},{8,10},{9,11},{10,... | collective-permute-start | bytes 294920 | tf_op jit(solution)/shard_map/while/body/eval_jaxpr/ppermute | solution.py:22
  126.5 2.7 collective-permute-start.6
  130.4 2.6 collective-permute-start.8
  134.6 4.4 %collective-permute-done.7 = bf16[32,1536]{1,0:T(8,128)(2,1)S(1)} collective-permute-done((bf16[32,1536]{1,0:T(8,128)(2,1)S(1)}, bf16[32,1536]{1,0:T(8,128)(2,1)S(1)}, u32[]{:S(2)}, u32[]{:S(2)}) %collective-permute-start.7) | collective-permute-done | bytes 98336 | tf_op jit(solution)/shard_map/while/body/eval_jaxpr/ppermute | solution.py:22
  143.3 3.0 collective-permute-start.1
  147.5 5.4 %fusion.50 = bf16[256,1536]{1,0:T(8,128)(2,1)} fusion(bf16[256,1536]{1,0:T(8,128)(2,1)S(1)} %get-tuple-element.339, bf16[1536,1536]{1,0:T(8,128)(2,1)} %get-tuple-element.409, bf16[256,1536]{1,0:T(8,128)(2,1)S(1)} %fusion.48, bf16[2,1536]{1,0:T(2,128)(2,1)S(1)} %collective-permute-done, bf16[2,1536]{1,0:T(2,128)(2,1)S(1)} %collective-permute-done.1, ...), kind=kOutput, calls=%fused_computation.10.clone.1 | convolution fusion | flops 1222901760 | bytes 7120896 | tf_op jit(solution)/shard_map/while/body/eval_jaxpr/dot_general | solution.py:59
  155.9 2.4 collective-permute-start.3
  159.5 5.5 %collective-permute-start.2 = (bf16[256,1536]{1,0:T(8,128)(2,1)}, bf16[256,1536]{1,0:T(8,128)(2,1)}, u32[]{:S(2)}, u32[]{:S(2)}) collective-permute-start(bf16[256,1536]{1,0:T(8,128)(2,1)} %fusion.50), channel_id=1, source_target_pairs={{0,8},{8,16},{16,24},{1,9},{9,17},{17,25},{2,10},{10,18},{18,26},{... | collective-permute-start | bytes 2359304 | tf_op jit(solution)/shard_map/while/body/eval_jaxpr/ppermute | solution.py:45
  165.0 3.1 %collective-permute-start.4 = (bf16[32,1536]{1,0:T(8,128)(2,1)}, bf16[32,1536]{1,0:T(8,128)(2,1)S(1)}, u32[]{:S(2)}, u32[]{:S(2)}) collective-permute-start(bf16[32,1536]{1,0:T(8,128)(2,1)} %get-tuple-element.350), channel_id=1, source_target_pairs={{0,2},{1,3},{2,0},{3,1},{4,6},{5,7},{6,4},{7,5},{8,10},{9,11},{10,... | collective-permute-start | bytes 294920 | tf_op jit(solution)/shard_map/while/body/eval_jaxpr/ppermute | solution.py:22
  168.1 2.7 collective-permute-start.6
  172.0 2.6 collective-permute-start.8
  176.2 4.4 %collective-permute-done.7 = bf16[32,1536]{1,0:T(8,128)(2,1)S(1)} collective-permute-done((bf16[32,1536]{1,0:T(8,128)(2,1)S(1)}, bf16[32,1536]{1,0:T(8,128)(2,1)S(1)}, u32[]{:S(2)}, u32[]{:S(2)}) %collective-permute-start.7) | collective-permute-done | bytes 98336 | tf_op jit(solution)/shard_map/while/body/eval_jaxpr/ppermute | solution.py:22
  184.9 3.0 collective-permute-start.1
  189.1 5.4 %fusion.50 = bf16[256,1536]{1,0:T(8,128)(2,1)} fusion(bf16[256,1536]{1,0:T(8,128)(2,1)S(1)} %get-tuple-element.339, bf16[1536,1536]{1,0:T(8,128)(2,1)} %get-tuple-element.409, bf16[256,1536]{1,0:T(8,128)(2,1)S(1)} %fusion.48, bf16[2,1536]{1,0:T(2,128)(2,1)S(1)} %collective-permute-done, bf16[2,1536]{1,0:T(2,128)(2,1)S(1)} %collective-permute-done.1, ...), kind=kOutput, calls=%fused_computation.10.clone.1 | convolution fusion | flops 1222901760 | bytes 7120896 | tf_op jit(solution)/shard_map/while/body/eval_jaxpr/dot_general | solution.py:59
  197.5 2.4 collective-permute-start.3
  201.1 5.5 %collective-permute-start.2 = (bf16[256,1536]{1,0:T(8,128)(2,1)}, bf16[256,1536]{1,0:T(8,128)(2,1)}, u32[]{:S(2)}, u32[]{:S(2)}) collective-permute-start(bf16[256,1536]{1,0:T(8,128)(2,1)} %fusion.50), channel_id=1, source_target_pairs={{0,8},{8,16},{16,24},{1,9},{9,17},{17,25},{2,10},{10,18},{18,26},{... | collective-permute-start | bytes 2359304 | tf_op jit(solution)/shard_map/while/body/eval_jaxpr/ppermute | solution.py:45
  206.6 3.1 %collective-permute-start.4 = (bf16[32,1536]{1,0:T(8,128)(2,1)}, bf16[32,1536]{1,0:T(8,128)(2,1)S(1)}, u32[]{:S(2)}, u32[]{:S(2)}) collective-permute-start(bf16[32,1536]{1,0:T(8,128)(2,1)} %get-tuple-element.350), channel_id=1, source_target_pairs={{0,2},{1,3},{2,0},{3,1},{4,6},{5,7},{6,4},{7,5},{8,10},{9,11},{10,... | collective-permute-start | bytes 294920 | tf_op jit(solution)/shard_map/while/body/eval_jaxpr/ppermute | solution.py:22
  209.7 2.7 collective-permute-start.6
  213.6 2.6 collective-permute-start.8
  217.8 4.4 %collective-permute-done.7 = bf16[32,1536]{1,0:T(8,128)(2,1)S(1)} collective-permute-done((bf16[32,1536]{1,0:T(8,128)(2,1)S(1)}, bf16[32,1536]{1,0:T(8,128)(2,1)S(1)}, u32[]{:S(2)}, u32[]{:S(2)}) %collective-permute-start.7) | collective-permute-done | bytes 98336 | tf_op jit(solution)/shard_map/while/body/eval_jaxpr/ppermute | solution.py:22
  226.5 3.0 collective-permute-start.1
  230.7 5.4 %fusion.50 = bf16[256,1536]{1,0:T(8,128)(2,1)} fusion(bf16[256,1536]{1,0:T(8,128)(2,1)S(1)} %get-tuple-element.339, bf16[1536,1536]{1,0:T(8,128)(2,1)} %get-tuple-element.409, bf16[256,1536]{1,0:T(8,128)(2,1)S(1)} %fusion.48, bf16[2,1536]{1,0:T(2,128)(2,1)S(1)} %collective-permute-done, bf16[2,1536]{1,0:T(2,128)(2,1)S(1)} %collective-permute-done.1, ...), kind=kOutput, calls=%fused_computation.10.clone.1 | convolution fusion | flops 1222901760 | bytes 7120896 | tf_op jit(solution)/shard_map/while/body/eval_jaxpr/dot_general | solution.py:59
  239.1 2.4 collective-permute-start.3
  242.7 5.5 %collective-permute-start.2 = (bf16[256,1536]{1,0:T(8,128)(2,1)}, bf16[256,1536]{1,0:T(8,128)(2,1)}, u32[]{:S(2)}, u32[]{:S(2)}) collective-permute-start(bf16[256,1536]{1,0:T(8,128)(2,1)} %fusion.50), channel_id=1, source_target_pairs={{0,8},{8,16},{16,24},{1,9},{9,17},{17,25},{2,10},{10,18},{18,26},{... | collective-permute-start | bytes 2359304 | tf_op jit(solution)/shard_map/while/body/eval_jaxpr/ppermute | solution.py:45
  248.2 3.1 %collective-permute-start.4 = (bf16[32,1536]{1,0:T(8,128)(2,1)}, bf16[32,1536]{1,0:T(8,128)(2,1)S(1)}, u32[]{:S(2)}, u32[]{:S(2)}) collective-permute-start(bf16[32,1536]{1,0:T(8,128)(2,1)} %get-tuple-element.350), channel_id=1, source_target_pairs={{0,2},{1,3},{2,0},{3,1},{4,6},{5,7},{6,4},{7,5},{8,10},{9,11},{10,... | collective-permute-start | bytes 294920 | tf_op jit(solution)/shard_map/while/body/eval_jaxpr/ppermute | solution.py:22
  251.4 2.7 collective-permute-start.6
  255.2 2.6 collective-permute-start.8
  259.4 4.4 %collective-permute-done.7 = bf16[32,1536]{1,0:T(8,128)(2,1)S(1)} collective-permute-done((bf16[32,1536]{1,0:T(8,128)(2,1)S(1)}, bf16[32,1536]{1,0:T(8,128)(2,1)S(1)}, u32[]{:S(2)}, u32[]{:S(2)}) %collective-permute-start.7) | collective-permute-done | bytes 98336 | tf_op jit(solution)/shard_map/while/body/eval_jaxpr/ppermute | solution.py:22
  268.1 3.0 collective-permute-start.1
  272.3 5.4 %fusion.50 = bf16[256,1536]{1,0:T(8,128)(2,1)} fusion(bf16[256,1536]{1,0:T(8,128)(2,1)S(1)} %get-tuple-element.339, bf16[1536,1536]{1,0:T(8,128)(2,1)} %get-tuple-element.409, bf16[256,1536]{1,0:T(8,128)(2,1)S(1)} %fusion.48, bf16[2,1536]{1,0:T(2,128)(2,1)S(1)} %collective-permute-done, bf16[2,1536]{1,0:T(2,128)(2,1)S(1)} %collective-permute-done.1, ...), kind=kOutput, calls=%fused_computation.10.clone.1 | convolution fusion | flops 1222901760 | bytes 7120896 | tf_op jit(solution)/shard_map/while/body/eval_jaxpr/dot_general | solution.py:59
  280.7 2.4 collective-permute-start.3
  284.3 5.5 %collective-permute-start.2 = (bf16[256,1536]{1,0:T(8,128)(2,1)}, bf16[256,1536]{1,0:T(8,128)(2,1)}, u32[]{:S(2)}, u32[]{:S(2)}) collective-permute-start(bf16[256,1536]{1,0:T(8,128)(2,1)} %fusion.50), channel_id=1, source_target_pairs={{0,8},{8,16},{16,24},{1,9},{9,17},{17,25},{2,10},{10,18},{18,26},{... | collective-permute-start | bytes 2359304 | tf_op jit(solution)/shard_map/while/body/eval_jaxpr/ppermute | solution.py:45
  289.8 3.1 %collective-permute-start.4 = (bf16[32,1536]{1,0:T(8,128)(2,1)}, bf16[32,1536]{1,0:T(8,128)(2,1)S(1)}, u32[]{:S(2)}, u32[]{:S(2)}) collective-permute-start(bf16[32,1536]{1,0:T(8,128)(2,1)} %get-tuple-element.350), channel_id=1, source_target_pairs={{0,2},{1,3},{2,0},{3,1},{4,6},{5,7},{6,4},{7,5},{8,10},{9,11},{10,... | collective-permute-start | bytes 294920 | tf_op jit(solution)/shard_map/while/body/eval_jaxpr/ppermute | solution.py:22
  293.0 2.7 collective-permute-start.6
  296.8 2.6 collective-permute-start.8
  299.5 1.5 collective-permute-start.9
  301.0 4.4 %collective-permute-done.7 = bf16[32,1536]{1,0:T(8,128)(2,1)S(1)} collective-permute-done((bf16[32,1536]{1,0:T(8,128)(2,1)S(1)}, bf16[32,1536]{1,0:T(8,128)(2,1)S(1)}, u32[]{:S(2)}, u32[]{:S(2)}) %collective-permute-start.7) | collective-permute-done | bytes 98336 | tf_op jit(solution)/shard_map/while/body/eval_jaxpr/ppermute | solution.py:22
  (239 shorter events, 85.7 us)
Async XLA Ops:
  18.6 5.5 %collective-permute-start = (bf16[2,1536]{1,0:T(2,128)(2,1)S(1)}, bf16[2,1536]{1,0:T(2,128)(2,1)S(1)}, u32[]{:S(2)}, u32[]{:S(2)}) collective-permute-start(bf16[2,1536]{1,0:T(2,128)(2,1)S(1)} %get-tuple-element.341), channel_id=1, source_target_pairs={{1,0},{2,1},{3,2},{4,3},{5,4},{6,5},{7,6},{9,8},{10,9},{11,10},{12... | collective-permute-start | bytes 18440 | tf_op jit(solution)/shard_map/while/body/eval_jaxpr/ppermute | solution.py:37
  19.9 4.2 %collective-permute-start.1 = (bf16[2,1536]{1,0:T(2,128)(2,1)S(1)}, bf16[2,1536]{1,0:T(2,128)(2,1)S(1)}, u32[]{:S(2)}, u32[]{:S(2)}) collective-permute-start(bf16[2,1536]{1,0:T(2,128)(2,1)S(1)} %get-tuple-element.342), channel_id=1, source_target_pairs={{0,1},{1,2},{2,3},{3,4},{4,5},{5,6},{6,7},{8,9},{9,10},{10,11},{11... | collective-permute-start | bytes 18440 | tf_op jit(solution)/shard_map/while/body/eval_jaxpr/ppermute | solution.py:34
  32.5 13.5 %collective-permute-start.3 = (bf16[32,1536]{1,0:T(8,128)(2,1)}, bf16[32,1536]{1,0:T(8,128)(2,1)}, u32[]{:S(2)}, u32[]{:S(2)}) collective-permute-start(bf16[32,1536]{1,0:T(8,128)(2,1)} %get-tuple-element.349), channel_id=1, source_target_pairs={{0,1},{1,0},{2,3},{3,2},{4,5},{5,4},{6,7},{7,6},{8,9},{9,8},{10,11... | collective-permute-start | bytes 294920 | tf_op jit(solution)/shard_map/while/body/eval_jaxpr/ppermute | solution.py:22
  36.3 21.0 %collective-permute-start.2 = (bf16[256,1536]{1,0:T(8,128)(2,1)}, bf16[256,1536]{1,0:T(8,128)(2,1)}, u32[]{:S(2)}, u32[]{:S(2)}) collective-permute-start(bf16[256,1536]{1,0:T(8,128)(2,1)} %fusion.50), channel_id=1, source_target_pairs={{0,8},{8,16},{16,24},{1,9},{9,17},{17,25},{2,10},{10,18},{18,26},{... | collective-permute-start | bytes 2359304 | tf_op jit(solution)/shard_map/while/body/eval_jaxpr/ppermute | solution.py:45
  40.9 6.2 %collective-permute-start.4 = (bf16[32,1536]{1,0:T(8,128)(2,1)}, bf16[32,1536]{1,0:T(8,128)(2,1)S(1)}, u32[]{:S(2)}, u32[]{:S(2)}) collective-permute-start(bf16[32,1536]{1,0:T(8,128)(2,1)} %get-tuple-element.350), channel_id=1, source_target_pairs={{0,2},{1,3},{2,0},{3,1},{4,6},{5,7},{6,4},{7,5},{8,10},{9,11},{10,... | collective-permute-start | bytes 294920 | tf_op jit(solution)/shard_map/while/body/eval_jaxpr/ppermute | solution.py:22
  43.3 6.2 %collective-permute-start.5 = (bf16[32,1536]{1,0:T(8,128)(2,1)}, bf16[32,1536]{1,0:T(8,128)(2,1)S(1)}, u32[]{:S(2)}, u32[]{:S(2)}) collective-permute-start(bf16[32,1536]{1,0:T(8,128)(2,1)} %get-tuple-element.351), channel_id=1, source_target_pairs={{0,3},{1,2},{2,1},{3,0},{4,7},{5,6},{6,5},{7,4},{8,11},{9,10},{10,... | collective-permute-start | bytes 294920 | tf_op jit(solution)/shard_map/while/body/eval_jaxpr/ppermute | solution.py:22
  43.3 7.9 %collective-permute-start.6 = (bf16[32,1536]{1,0:T(8,128)(2,1)S(1)}, bf16[32,1536]{1,0:T(8,128)(2,1)S(1)}, u32[]{:S(2)}, u32[]{:S(2)}) collective-permute-start(bf16[32,1536]{1,0:T(8,128)(2,1)S(1)} %get-tuple-element.352), channel_id=1, source_target_pairs={{0,4},{1,5},{2,6},{3,7},{4,0},{5,1},{6,2},{7,3},{8,12},{9,13},{10,... | collective-permute-start | bytes 294920 | tf_op jit(solution)/shard_map/while/body/eval_jaxpr/ppermute | solution.py:22
  46.0 9.7 %collective-permute-start.7 = (bf16[32,1536]{1,0:T(8,128)(2,1)S(1)}, bf16[32,1536]{1,0:T(8,128)(2,1)S(1)}, u32[]{:S(2)}, u32[]{:S(2)}) collective-permute-start(bf16[32,1536]{1,0:T(8,128)(2,1)S(1)} %get-tuple-element.353), channel_id=1, source_target_pairs={{0,5},{1,4},{2,7},{3,6},{4,1},{5,0},{6,3},{7,2},{8,13},{9,12},{10,... | collective-permute-start | bytes 294920 | tf_op jit(solution)/shard_map/while/body/eval_jaxpr/ppermute | solution.py:22
  47.1 8.6 %collective-permute-start.8 = (bf16[32,1536]{1,0:T(8,128)(2,1)S(1)}, bf16[32,1536]{1,0:T(8,128)(2,1)S(1)}, u32[]{:S(2)}, u32[]{:S(2)}) collective-permute-start(bf16[32,1536]{1,0:T(8,128)(2,1)S(1)} %get-tuple-element.354), channel_id=1, source_target_pairs={{0,6},{1,7},{2,4},{3,5},{4,2},{5,3},{6,0},{7,1},{8,14},{9,15},{10,... | collective-permute-start | bytes 294920 | tf_op jit(solution)/shard_map/while/body/eval_jaxpr/ppermute | solution.py:22
  49.5 6.3 %collective-permute-start.9 = (bf16[32,1536]{1,0:T(8,128)(2,1)S(1)}, bf16[32,1536]{1,0:T(8,128)(2,1)S(1)}, u32[]{:S(2)}, u32[]{:S(2)}) collective-permute-start(bf16[32,1536]{1,0:T(8,128)(2,1)S(1)} %get-tuple-element.355), channel_id=1, source_target_pairs={{0,7},{1,6},{2,5},{3,4},{4,3},{5,2},{6,1},{7,0},{8,15},{9,14},{10,... | collective-permute-start | bytes 294920 | tf_op jit(solution)/shard_map/while/body/eval_jaxpr/ppermute | solution.py:22
  59.1 5.5 %collective-permute-start = (bf16[2,1536]{1,0:T(2,128)(2,1)S(1)}, bf16[2,1536]{1,0:T(2,128)(2,1)S(1)}, u32[]{:S(2)}, u32[]{:S(2)}) collective-permute-start(bf16[2,1536]{1,0:T(2,128)(2,1)S(1)} %get-tuple-element.341), channel_id=1, source_target_pairs={{1,0},{2,1},{3,2},{4,3},{5,4},{6,5},{7,6},{9,8},{10,9},{11,10},{12... | collective-permute-start | bytes 18440 | tf_op jit(solution)/shard_map/while/body/eval_jaxpr/ppermute | solution.py:37
  73.0 14.6 %collective-permute-start.3 = (bf16[32,1536]{1,0:T(8,128)(2,1)}, bf16[32,1536]{1,0:T(8,128)(2,1)}, u32[]{:S(2)}, u32[]{:S(2)}) collective-permute-start(bf16[32,1536]{1,0:T(8,128)(2,1)} %get-tuple-element.349), channel_id=1, source_target_pairs={{0,1},{1,0},{2,3},{3,2},{4,5},{5,4},{6,7},{7,6},{8,9},{9,8},{10,11... | collective-permute-start | bytes 294920 | tf_op jit(solution)/shard_map/while/body/eval_jaxpr/ppermute | solution.py:22
  76.2 22.3 %collective-permute-start.2 = (bf16[256,1536]{1,0:T(8,128)(2,1)}, bf16[256,1536]{1,0:T(8,128)(2,1)}, u32[]{:S(2)}, u32[]{:S(2)}) collective-permute-start(bf16[256,1536]{1,0:T(8,128)(2,1)} %fusion.50), channel_id=1, source_target_pairs={{0,8},{8,16},{16,24},{1,9},{9,17},{17,25},{2,10},{10,18},{18,26},{... | collective-permute-start | bytes 2359304 | tf_op jit(solution)/shard_map/while/body/eval_jaxpr/ppermute | solution.py:45
  81.7 7.0 %collective-permute-start.4 = (bf16[32,1536]{1,0:T(8,128)(2,1)}, bf16[32,1536]{1,0:T(8,128)(2,1)S(1)}, u32[]{:S(2)}, u32[]{:S(2)}) collective-permute-start(bf16[32,1536]{1,0:T(8,128)(2,1)} %get-tuple-element.350), channel_id=1, source_target_pairs={{0,2},{1,3},{2,0},{3,1},{4,6},{5,7},{6,4},{7,5},{8,10},{9,11},{10,... | collective-permute-start | bytes 294920 | tf_op jit(solution)/shard_map/while/body/eval_jaxpr/ppermute | solution.py:22
  84.9 6.5 %collective-permute-start.5 = (bf16[32,1536]{1,0:T(8,128)(2,1)}, bf16[32,1536]{1,0:T(8,128)(2,1)S(1)}, u32[]{:S(2)}, u32[]{:S(2)}) collective-permute-start(bf16[32,1536]{1,0:T(8,128)(2,1)} %get-tuple-element.351), channel_id=1, source_target_pairs={{0,3},{1,2},{2,1},{3,0},{4,7},{5,6},{6,5},{7,4},{8,11},{9,10},{10,... | collective-permute-start | bytes 294920 | tf_op jit(solution)/shard_map/while/body/eval_jaxpr/ppermute | solution.py:22
  84.9 8.0 %collective-permute-start.6 = (bf16[32,1536]{1,0:T(8,128)(2,1)S(1)}, bf16[32,1536]{1,0:T(8,128)(2,1)S(1)}, u32[]{:S(2)}, u32[]{:S(2)}) collective-permute-start(bf16[32,1536]{1,0:T(8,128)(2,1)S(1)} %get-tuple-element.352), channel_id=1, source_target_pairs={{0,4},{1,5},{2,6},{3,7},{4,0},{5,1},{6,2},{7,3},{8,12},{9,13},{10,... | collective-permute-start | bytes 294920 | tf_op jit(solution)/shard_map/while/body/eval_jaxpr/ppermute | solution.py:22
  87.6 9.7 %collective-permute-start.7 = (bf16[32,1536]{1,0:T(8,128)(2,1)S(1)}, bf16[32,1536]{1,0:T(8,128)(2,1)S(1)}, u32[]{:S(2)}, u32[]{:S(2)}) collective-permute-start(bf16[32,1536]{1,0:T(8,128)(2,1)S(1)} %get-tuple-element.353), channel_id=1, source_target_pairs={{0,5},{1,4},{2,7},{3,6},{4,1},{5,0},{6,3},{7,2},{8,13},{9,12},{10,... | collective-permute-start | bytes 294920 | tf_op jit(solution)/shard_map/while/body/eval_jaxpr/ppermute | solution.py:22
  88.8 8.6 %collective-permute-start.8 = (bf16[32,1536]{1,0:T(8,128)(2,1)S(1)}, bf16[32,1536]{1,0:T(8,128)(2,1)S(1)}, u32[]{:S(2)}, u32[]{:S(2)}) collective-permute-start(bf16[32,1536]{1,0:T(8,128)(2,1)S(1)} %get-tuple-element.354), channel_id=1, source_target_pairs={{0,6},{1,7},{2,4},{3,5},{4,2},{5,3},{6,0},{7,1},{8,14},{9,15},{10,... | collective-permute-start | bytes 294920 | tf_op jit(solution)/shard_map/while/body/eval_jaxpr/ppermute | solution.py:22
  91.4 6.0 %collective-permute-start.9 = (bf16[32,1536]{1,0:T(8,128)(2,1)S(1)}, bf16[32,1536]{1,0:T(8,128)(2,1)S(1)}, u32[]{:S(2)}, u32[]{:S(2)}) collective-permute-start(bf16[32,1536]{1,0:T(8,128)(2,1)S(1)} %get-tuple-element.355), channel_id=1, source_target_pairs={{0,7},{1,6},{2,5},{3,4},{4,3},{5,2},{6,1},{7,0},{8,15},{9,14},{10,... | collective-permute-start | bytes 294920 | tf_op jit(solution)/shard_map/while/body/eval_jaxpr/ppermute | solution.py:22
  100.3 5.5 %collective-permute-start = (bf16[2,1536]{1,0:T(2,128)(2,1)S(1)}, bf16[2,1536]{1,0:T(2,128)(2,1)S(1)}, u32[]{:S(2)}, u32[]{:S(2)}) collective-permute-start(bf16[2,1536]{1,0:T(2,128)(2,1)S(1)} %get-tuple-element.341), channel_id=1, source_target_pairs={{1,0},{2,1},{3,2},{4,3},{5,4},{6,5},{7,6},{9,8},{10,9},{11,10},{12... | collective-permute-start | bytes 18440 | tf_op jit(solution)/shard_map/while/body/eval_jaxpr/ppermute | solution.py:37
  114.3 15.0 %collective-permute-start.3 = (bf16[32,1536]{1,0:T(8,128)(2,1)}, bf16[32,1536]{1,0:T(8,128)(2,1)}, u32[]{:S(2)}, u32[]{:S(2)}) collective-permute-start(bf16[32,1536]{1,0:T(8,128)(2,1)} %get-tuple-element.349), channel_id=1, source_target_pairs={{0,1},{1,0},{2,3},{3,2},{4,5},{5,4},{6,7},{7,6},{8,9},{9,8},{10,11... | collective-permute-start | bytes 294920 | tf_op jit(solution)/shard_map/while/body/eval_jaxpr/ppermute | solution.py:22
  117.8 22.3 %collective-permute-start.2 = (bf16[256,1536]{1,0:T(8,128)(2,1)}, bf16[256,1536]{1,0:T(8,128)(2,1)}, u32[]{:S(2)}, u32[]{:S(2)}) collective-permute-start(bf16[256,1536]{1,0:T(8,128)(2,1)} %fusion.50), channel_id=1, source_target_pairs={{0,8},{8,16},{16,24},{1,9},{9,17},{17,25},{2,10},{10,18},{18,26},{... | collective-permute-start | bytes 2359304 | tf_op jit(solution)/shard_map/while/body/eval_jaxpr/ppermute | solution.py:45
  123.4 7.0 %collective-permute-start.4 = (bf16[32,1536]{1,0:T(8,128)(2,1)}, bf16[32,1536]{1,0:T(8,128)(2,1)S(1)}, u32[]{:S(2)}, u32[]{:S(2)}) collective-permute-start(bf16[32,1536]{1,0:T(8,128)(2,1)} %get-tuple-element.350), channel_id=1, source_target_pairs={{0,2},{1,3},{2,0},{3,1},{4,6},{5,7},{6,4},{7,5},{8,10},{9,11},{10,... | collective-permute-start | bytes 294920 | tf_op jit(solution)/shard_map/while/body/eval_jaxpr/ppermute | solution.py:22
  126.5 6.5 %collective-permute-start.5 = (bf16[32,1536]{1,0:T(8,128)(2,1)}, bf16[32,1536]{1,0:T(8,128)(2,1)S(1)}, u32[]{:S(2)}, u32[]{:S(2)}) collective-permute-start(bf16[32,1536]{1,0:T(8,128)(2,1)} %get-tuple-element.351), channel_id=1, source_target_pairs={{0,3},{1,2},{2,1},{3,0},{4,7},{5,6},{6,5},{7,4},{8,11},{9,10},{10,... | collective-permute-start | bytes 294920 | tf_op jit(solution)/shard_map/while/body/eval_jaxpr/ppermute | solution.py:22
  126.5 8.0 %collective-permute-start.6 = (bf16[32,1536]{1,0:T(8,128)(2,1)S(1)}, bf16[32,1536]{1,0:T(8,128)(2,1)S(1)}, u32[]{:S(2)}, u32[]{:S(2)}) collective-permute-start(bf16[32,1536]{1,0:T(8,128)(2,1)S(1)} %get-tuple-element.352), channel_id=1, source_target_pairs={{0,4},{1,5},{2,6},{3,7},{4,0},{5,1},{6,2},{7,3},{8,12},{9,13},{10,... | collective-permute-start | bytes 294920 | tf_op jit(solution)/shard_map/while/body/eval_jaxpr/ppermute | solution.py:22
  129.3 9.7 %collective-permute-start.7 = (bf16[32,1536]{1,0:T(8,128)(2,1)S(1)}, bf16[32,1536]{1,0:T(8,128)(2,1)S(1)}, u32[]{:S(2)}, u32[]{:S(2)}) collective-permute-start(bf16[32,1536]{1,0:T(8,128)(2,1)S(1)} %get-tuple-element.353), channel_id=1, source_target_pairs={{0,5},{1,4},{2,7},{3,6},{4,1},{5,0},{6,3},{7,2},{8,13},{9,12},{10,... | collective-permute-start | bytes 294920 | tf_op jit(solution)/shard_map/while/body/eval_jaxpr/ppermute | solution.py:22
  130.4 8.6 %collective-permute-start.8 = (bf16[32,1536]{1,0:T(8,128)(2,1)S(1)}, bf16[32,1536]{1,0:T(8,128)(2,1)S(1)}, u32[]{:S(2)}, u32[]{:S(2)}) collective-permute-start(bf16[32,1536]{1,0:T(8,128)(2,1)S(1)} %get-tuple-element.354), channel_id=1, source_target_pairs={{0,6},{1,7},{2,4},{3,5},{4,2},{5,3},{6,0},{7,1},{8,14},{9,15},{10,... | collective-permute-start | bytes 294920 | tf_op jit(solution)/shard_map/while/body/eval_jaxpr/ppermute | solution.py:22
  133.0 6.0 %collective-permute-start.9 = (bf16[32,1536]{1,0:T(8,128)(2,1)S(1)}, bf16[32,1536]{1,0:T(8,128)(2,1)S(1)}, u32[]{:S(2)}, u32[]{:S(2)}) collective-permute-start(bf16[32,1536]{1,0:T(8,128)(2,1)S(1)} %get-tuple-element.355), channel_id=1, source_target_pairs={{0,7},{1,6},{2,5},{3,4},{4,3},{5,2},{6,1},{7,0},{8,15},{9,14},{10,... | collective-permute-start | bytes 294920 | tf_op jit(solution)/shard_map/while/body/eval_jaxpr/ppermute | solution.py:22
  142.0 5.5 %collective-permute-start = (bf16[2,1536]{1,0:T(2,128)(2,1)S(1)}, bf16[2,1536]{1,0:T(2,128)(2,1)S(1)}, u32[]{:S(2)}, u32[]{:S(2)}) collective-permute-start(bf16[2,1536]{1,0:T(2,128)(2,1)S(1)} %get-tuple-element.341), channel_id=1, source_target_pairs={{1,0},{2,1},{3,2},{4,3},{5,4},{6,5},{7,6},{9,8},{10,9},{11,10},{12... | collective-permute-start | bytes 18440 | tf_op jit(solution)/shard_map/while/body/eval_jaxpr/ppermute | solution.py:37
  155.9 15.0 %collective-permute-start.3 = (bf16[32,1536]{1,0:T(8,128)(2,1)}, bf16[32,1536]{1,0:T(8,128)(2,1)}, u32[]{:S(2)}, u32[]{:S(2)}) collective-permute-start(bf16[32,1536]{1,0:T(8,128)(2,1)} %get-tuple-element.349), channel_id=1, source_target_pairs={{0,1},{1,0},{2,3},{3,2},{4,5},{5,4},{6,7},{7,6},{8,9},{9,8},{10,11... | collective-permute-start | bytes 294920 | tf_op jit(solution)/shard_map/while/body/eval_jaxpr/ppermute | solution.py:22
  159.5 22.3 %collective-permute-start.2 = (bf16[256,1536]{1,0:T(8,128)(2,1)}, bf16[256,1536]{1,0:T(8,128)(2,1)}, u32[]{:S(2)}, u32[]{:S(2)}) collective-permute-start(bf16[256,1536]{1,0:T(8,128)(2,1)} %fusion.50), channel_id=1, source_target_pairs={{0,8},{8,16},{16,24},{1,9},{9,17},{17,25},{2,10},{10,18},{18,26},{... | collective-permute-start | bytes 2359304 | tf_op jit(solution)/shard_map/while/body/eval_jaxpr/ppermute | solution.py:45
  165.0 7.0 %collective-permute-start.4 = (bf16[32,1536]{1,0:T(8,128)(2,1)}, bf16[32,1536]{1,0:T(8,128)(2,1)S(1)}, u32[]{:S(2)}, u32[]{:S(2)}) collective-permute-start(bf16[32,1536]{1,0:T(8,128)(2,1)} %get-tuple-element.350), channel_id=1, source_target_pairs={{0,2},{1,3},{2,0},{3,1},{4,6},{5,7},{6,4},{7,5},{8,10},{9,11},{10,... | collective-permute-start | bytes 294920 | tf_op jit(solution)/shard_map/while/body/eval_jaxpr/ppermute | solution.py:22
  168.1 6.5 %collective-permute-start.5 = (bf16[32,1536]{1,0:T(8,128)(2,1)}, bf16[32,1536]{1,0:T(8,128)(2,1)S(1)}, u32[]{:S(2)}, u32[]{:S(2)}) collective-permute-start(bf16[32,1536]{1,0:T(8,128)(2,1)} %get-tuple-element.351), channel_id=1, source_target_pairs={{0,3},{1,2},{2,1},{3,0},{4,7},{5,6},{6,5},{7,4},{8,11},{9,10},{10,... | collective-permute-start | bytes 294920 | tf_op jit(solution)/shard_map/while/body/eval_jaxpr/ppermute | solution.py:22
  168.1 8.0 %collective-permute-start.6 = (bf16[32,1536]{1,0:T(8,128)(2,1)S(1)}, bf16[32,1536]{1,0:T(8,128)(2,1)S(1)}, u32[]{:S(2)}, u32[]{:S(2)}) collective-permute-start(bf16[32,1536]{1,0:T(8,128)(2,1)S(1)} %get-tuple-element.352), channel_id=1, source_target_pairs={{0,4},{1,5},{2,6},{3,7},{4,0},{5,1},{6,2},{7,3},{8,12},{9,13},{10,... | collective-permute-start | bytes 294920 | tf_op jit(solution)/shard_map/while/body/eval_jaxpr/ppermute | solution.py:22
  170.9 9.7 %collective-permute-start.7 = (bf16[32,1536]{1,0:T(8,128)(2,1)S(1)}, bf16[32,1536]{1,0:T(8,128)(2,1)S(1)}, u32[]{:S(2)}, u32[]{:S(2)}) collective-permute-start(bf16[32,1536]{1,0:T(8,128)(2,1)S(1)} %get-tuple-element.353), channel_id=1, source_target_pairs={{0,5},{1,4},{2,7},{3,6},{4,1},{5,0},{6,3},{7,2},{8,13},{9,12},{10,... | collective-permute-start | bytes 294920 | tf_op jit(solution)/shard_map/while/body/eval_jaxpr/ppermute | solution.py:22
  172.0 8.6 %collective-permute-start.8 = (bf16[32,1536]{1,0:T(8,128)(2,1)S(1)}, bf16[32,1536]{1,0:T(8,128)(2,1)S(1)}, u32[]{:S(2)}, u32[]{:S(2)}) collective-permute-start(bf16[32,1536]{1,0:T(8,128)(2,1)S(1)} %get-tuple-element.354), channel_id=1, source_target_pairs={{0,6},{1,7},{2,4},{3,5},{4,2},{5,3},{6,0},{7,1},{8,14},{9,15},{10,... | collective-permute-start | bytes 294920 | tf_op jit(solution)/shard_map/while/body/eval_jaxpr/ppermute | solution.py:22
  174.6 6.0 %collective-permute-start.9 = (bf16[32,1536]{1,0:T(8,128)(2,1)S(1)}, bf16[32,1536]{1,0:T(8,128)(2,1)S(1)}, u32[]{:S(2)}, u32[]{:S(2)}) collective-permute-start(bf16[32,1536]{1,0:T(8,128)(2,1)S(1)} %get-tuple-element.355), channel_id=1, source_target_pairs={{0,7},{1,6},{2,5},{3,4},{4,3},{5,2},{6,1},{7,0},{8,15},{9,14},{10,... | collective-permute-start | bytes 294920 | tf_op jit(solution)/shard_map/while/body/eval_jaxpr/ppermute | solution.py:22
  183.6 5.5 %collective-permute-start = (bf16[2,1536]{1,0:T(2,128)(2,1)S(1)}, bf16[2,1536]{1,0:T(2,128)(2,1)S(1)}, u32[]{:S(2)}, u32[]{:S(2)}) collective-permute-start(bf16[2,1536]{1,0:T(2,128)(2,1)S(1)} %get-tuple-element.341), channel_id=1, source_target_pairs={{1,0},{2,1},{3,2},{4,3},{5,4},{6,5},{7,6},{9,8},{10,9},{11,10},{12... | collective-permute-start | bytes 18440 | tf_op jit(solution)/shard_map/while/body/eval_jaxpr/ppermute | solution.py:37
  197.5 15.0 %collective-permute-start.3 = (bf16[32,1536]{1,0:T(8,128)(2,1)}, bf16[32,1536]{1,0:T(8,128)(2,1)}, u32[]{:S(2)}, u32[]{:S(2)}) collective-permute-start(bf16[32,1536]{1,0:T(8,128)(2,1)} %get-tuple-element.349), channel_id=1, source_target_pairs={{0,1},{1,0},{2,3},{3,2},{4,5},{5,4},{6,7},{7,6},{8,9},{9,8},{10,11... | collective-permute-start | bytes 294920 | tf_op jit(solution)/shard_map/while/body/eval_jaxpr/ppermute | solution.py:22
  201.1 22.3 %collective-permute-start.2 = (bf16[256,1536]{1,0:T(8,128)(2,1)}, bf16[256,1536]{1,0:T(8,128)(2,1)}, u32[]{:S(2)}, u32[]{:S(2)}) collective-permute-start(bf16[256,1536]{1,0:T(8,128)(2,1)} %fusion.50), channel_id=1, source_target_pairs={{0,8},{8,16},{16,24},{1,9},{9,17},{17,25},{2,10},{10,18},{18,26},{... | collective-permute-start | bytes 2359304 | tf_op jit(solution)/shard_map/while/body/eval_jaxpr/ppermute | solution.py:45
  206.6 7.0 %collective-permute-start.4 = (bf16[32,1536]{1,0:T(8,128)(2,1)}, bf16[32,1536]{1,0:T(8,128)(2,1)S(1)}, u32[]{:S(2)}, u32[]{:S(2)}) collective-permute-start(bf16[32,1536]{1,0:T(8,128)(2,1)} %get-tuple-element.350), channel_id=1, source_target_pairs={{0,2},{1,3},{2,0},{3,1},{4,6},{5,7},{6,4},{7,5},{8,10},{9,11},{10,... | collective-permute-start | bytes 294920 | tf_op jit(solution)/shard_map/while/body/eval_jaxpr/ppermute | solution.py:22
  209.7 6.5 %collective-permute-start.5 = (bf16[32,1536]{1,0:T(8,128)(2,1)}, bf16[32,1536]{1,0:T(8,128)(2,1)S(1)}, u32[]{:S(2)}, u32[]{:S(2)}) collective-permute-start(bf16[32,1536]{1,0:T(8,128)(2,1)} %get-tuple-element.351), channel_id=1, source_target_pairs={{0,3},{1,2},{2,1},{3,0},{4,7},{5,6},{6,5},{7,4},{8,11},{9,10},{10,... | collective-permute-start | bytes 294920 | tf_op jit(solution)/shard_map/while/body/eval_jaxpr/ppermute | solution.py:22
  209.7 8.0 %collective-permute-start.6 = (bf16[32,1536]{1,0:T(8,128)(2,1)S(1)}, bf16[32,1536]{1,0:T(8,128)(2,1)S(1)}, u32[]{:S(2)}, u32[]{:S(2)}) collective-permute-start(bf16[32,1536]{1,0:T(8,128)(2,1)S(1)} %get-tuple-element.352), channel_id=1, source_target_pairs={{0,4},{1,5},{2,6},{3,7},{4,0},{5,1},{6,2},{7,3},{8,12},{9,13},{10,... | collective-permute-start | bytes 294920 | tf_op jit(solution)/shard_map/while/body/eval_jaxpr/ppermute | solution.py:22
  212.5 9.7 %collective-permute-start.7 = (bf16[32,1536]{1,0:T(8,128)(2,1)S(1)}, bf16[32,1536]{1,0:T(8,128)(2,1)S(1)}, u32[]{:S(2)}, u32[]{:S(2)}) collective-permute-start(bf16[32,1536]{1,0:T(8,128)(2,1)S(1)} %get-tuple-element.353), channel_id=1, source_target_pairs={{0,5},{1,4},{2,7},{3,6},{4,1},{5,0},{6,3},{7,2},{8,13},{9,12},{10,... | collective-permute-start | bytes 294920 | tf_op jit(solution)/shard_map/while/body/eval_jaxpr/ppermute | solution.py:22
  213.6 8.6 %collective-permute-start.8 = (bf16[32,1536]{1,0:T(8,128)(2,1)S(1)}, bf16[32,1536]{1,0:T(8,128)(2,1)S(1)}, u32[]{:S(2)}, u32[]{:S(2)}) collective-permute-start(bf16[32,1536]{1,0:T(8,128)(2,1)S(1)} %get-tuple-element.354), channel_id=1, source_target_pairs={{0,6},{1,7},{2,4},{3,5},{4,2},{5,3},{6,0},{7,1},{8,14},{9,15},{10,... | collective-permute-start | bytes 294920 | tf_op jit(solution)/shard_map/while/body/eval_jaxpr/ppermute | solution.py:22
  216.3 6.0 %collective-permute-start.9 = (bf16[32,1536]{1,0:T(8,128)(2,1)S(1)}, bf16[32,1536]{1,0:T(8,128)(2,1)S(1)}, u32[]{:S(2)}, u32[]{:S(2)}) collective-permute-start(bf16[32,1536]{1,0:T(8,128)(2,1)S(1)} %get-tuple-element.355), channel_id=1, source_target_pairs={{0,7},{1,6},{2,5},{3,4},{4,3},{5,2},{6,1},{7,0},{8,15},{9,14},{10,... | collective-permute-start | bytes 294920 | tf_op jit(solution)/shard_map/while/body/eval_jaxpr/ppermute | solution.py:22
  225.2 5.5 %collective-permute-start = (bf16[2,1536]{1,0:T(2,128)(2,1)S(1)}, bf16[2,1536]{1,0:T(2,128)(2,1)S(1)}, u32[]{:S(2)}, u32[]{:S(2)}) collective-permute-start(bf16[2,1536]{1,0:T(2,128)(2,1)S(1)} %get-tuple-element.341), channel_id=1, source_target_pairs={{1,0},{2,1},{3,2},{4,3},{5,4},{6,5},{7,6},{9,8},{10,9},{11,10},{12... | collective-permute-start | bytes 18440 | tf_op jit(solution)/shard_map/while/body/eval_jaxpr/ppermute | solution.py:37
  239.1 15.0 %collective-permute-start.3 = (bf16[32,1536]{1,0:T(8,128)(2,1)}, bf16[32,1536]{1,0:T(8,128)(2,1)}, u32[]{:S(2)}, u32[]{:S(2)}) collective-permute-start(bf16[32,1536]{1,0:T(8,128)(2,1)} %get-tuple-element.349), channel_id=1, source_target_pairs={{0,1},{1,0},{2,3},{3,2},{4,5},{5,4},{6,7},{7,6},{8,9},{9,8},{10,11... | collective-permute-start | bytes 294920 | tf_op jit(solution)/shard_map/while/body/eval_jaxpr/ppermute | solution.py:22
  242.7 22.3 %collective-permute-start.2 = (bf16[256,1536]{1,0:T(8,128)(2,1)}, bf16[256,1536]{1,0:T(8,128)(2,1)}, u32[]{:S(2)}, u32[]{:S(2)}) collective-permute-start(bf16[256,1536]{1,0:T(8,128)(2,1)} %fusion.50), channel_id=1, source_target_pairs={{0,8},{8,16},{16,24},{1,9},{9,17},{17,25},{2,10},{10,18},{18,26},{... | collective-permute-start | bytes 2359304 | tf_op jit(solution)/shard_map/while/body/eval_jaxpr/ppermute | solution.py:45
  248.2 7.0 %collective-permute-start.4 = (bf16[32,1536]{1,0:T(8,128)(2,1)}, bf16[32,1536]{1,0:T(8,128)(2,1)S(1)}, u32[]{:S(2)}, u32[]{:S(2)}) collective-permute-start(bf16[32,1536]{1,0:T(8,128)(2,1)} %get-tuple-element.350), channel_id=1, source_target_pairs={{0,2},{1,3},{2,0},{3,1},{4,6},{5,7},{6,4},{7,5},{8,10},{9,11},{10,... | collective-permute-start | bytes 294920 | tf_op jit(solution)/shard_map/while/body/eval_jaxpr/ppermute | solution.py:22
  251.3 6.5 %collective-permute-start.5 = (bf16[32,1536]{1,0:T(8,128)(2,1)}, bf16[32,1536]{1,0:T(8,128)(2,1)S(1)}, u32[]{:S(2)}, u32[]{:S(2)}) collective-permute-start(bf16[32,1536]{1,0:T(8,128)(2,1)} %get-tuple-element.351), channel_id=1, source_target_pairs={{0,3},{1,2},{2,1},{3,0},{4,7},{5,6},{6,5},{7,4},{8,11},{9,10},{10,... | collective-permute-start | bytes 294920 | tf_op jit(solution)/shard_map/while/body/eval_jaxpr/ppermute | solution.py:22
  251.4 8.0 %collective-permute-start.6 = (bf16[32,1536]{1,0:T(8,128)(2,1)S(1)}, bf16[32,1536]{1,0:T(8,128)(2,1)S(1)}, u32[]{:S(2)}, u32[]{:S(2)}) collective-permute-start(bf16[32,1536]{1,0:T(8,128)(2,1)S(1)} %get-tuple-element.352), channel_id=1, source_target_pairs={{0,4},{1,5},{2,6},{3,7},{4,0},{5,1},{6,2},{7,3},{8,12},{9,13},{10,... | collective-permute-start | bytes 294920 | tf_op jit(solution)/shard_map/while/body/eval_jaxpr/ppermute | solution.py:22
  254.1 9.7 %collective-permute-start.7 = (bf16[32,1536]{1,0:T(8,128)(2,1)S(1)}, bf16[32,1536]{1,0:T(8,128)(2,1)S(1)}, u32[]{:S(2)}, u32[]{:S(2)}) collective-permute-start(bf16[32,1536]{1,0:T(8,128)(2,1)S(1)} %get-tuple-element.353), channel_id=1, source_target_pairs={{0,5},{1,4},{2,7},{3,6},{4,1},{5,0},{6,3},{7,2},{8,13},{9,12},{10,... | collective-permute-start | bytes 294920 | tf_op jit(solution)/shard_map/while/body/eval_jaxpr/ppermute | solution.py:22
  255.2 8.6 %collective-permute-start.8 = (bf16[32,1536]{1,0:T(8,128)(2,1)S(1)}, bf16[32,1536]{1,0:T(8,128)(2,1)S(1)}, u32[]{:S(2)}, u32[]{:S(2)}) collective-permute-start(bf16[32,1536]{1,0:T(8,128)(2,1)S(1)} %get-tuple-element.354), channel_id=1, source_target_pairs={{0,6},{1,7},{2,4},{3,5},{4,2},{5,3},{6,0},{7,1},{8,14},{9,15},{10,... | collective-permute-start | bytes 294920 | tf_op jit(solution)/shard_map/while/body/eval_jaxpr/ppermute | solution.py:22
  257.9 6.0 %collective-permute-start.9 = (bf16[32,1536]{1,0:T(8,128)(2,1)S(1)}, bf16[32,1536]{1,0:T(8,128)(2,1)S(1)}, u32[]{:S(2)}, u32[]{:S(2)}) collective-permute-start(bf16[32,1536]{1,0:T(8,128)(2,1)S(1)} %get-tuple-element.355), channel_id=1, source_target_pairs={{0,7},{1,6},{2,5},{3,4},{4,3},{5,2},{6,1},{7,0},{8,15},{9,14},{10,... | collective-permute-start | bytes 294920 | tf_op jit(solution)/shard_map/while/body/eval_jaxpr/ppermute | solution.py:22
  266.8 5.5 %collective-permute-start = (bf16[2,1536]{1,0:T(2,128)(2,1)S(1)}, bf16[2,1536]{1,0:T(2,128)(2,1)S(1)}, u32[]{:S(2)}, u32[]{:S(2)}) collective-permute-start(bf16[2,1536]{1,0:T(2,128)(2,1)S(1)} %get-tuple-element.341), channel_id=1, source_target_pairs={{1,0},{2,1},{3,2},{4,3},{5,4},{6,5},{7,6},{9,8},{10,9},{11,10},{12... | collective-permute-start | bytes 18440 | tf_op jit(solution)/shard_map/while/body/eval_jaxpr/ppermute | solution.py:37
  280.7 15.0 %collective-permute-start.3 = (bf16[32,1536]{1,0:T(8,128)(2,1)}, bf16[32,1536]{1,0:T(8,128)(2,1)}, u32[]{:S(2)}, u32[]{:S(2)}) collective-permute-start(bf16[32,1536]{1,0:T(8,128)(2,1)} %get-tuple-element.349), channel_id=1, source_target_pairs={{0,1},{1,0},{2,3},{3,2},{4,5},{5,4},{6,7},{7,6},{8,9},{9,8},{10,11... | collective-permute-start | bytes 294920 | tf_op jit(solution)/shard_map/while/body/eval_jaxpr/ppermute | solution.py:22
  284.3 22.3 %collective-permute-start.2 = (bf16[256,1536]{1,0:T(8,128)(2,1)}, bf16[256,1536]{1,0:T(8,128)(2,1)}, u32[]{:S(2)}, u32[]{:S(2)}) collective-permute-start(bf16[256,1536]{1,0:T(8,128)(2,1)} %fusion.50), channel_id=1, source_target_pairs={{0,8},{8,16},{16,24},{1,9},{9,17},{17,25},{2,10},{10,18},{18,26},{... | collective-permute-start | bytes 2359304 | tf_op jit(solution)/shard_map/while/body/eval_jaxpr/ppermute | solution.py:45
  289.8 7.0 %collective-permute-start.4 = (bf16[32,1536]{1,0:T(8,128)(2,1)}, bf16[32,1536]{1,0:T(8,128)(2,1)S(1)}, u32[]{:S(2)}, u32[]{:S(2)}) collective-permute-start(bf16[32,1536]{1,0:T(8,128)(2,1)} %get-tuple-element.350), channel_id=1, source_target_pairs={{0,2},{1,3},{2,0},{3,1},{4,6},{5,7},{6,4},{7,5},{8,10},{9,11},{10,... | collective-permute-start | bytes 294920 | tf_op jit(solution)/shard_map/while/body/eval_jaxpr/ppermute | solution.py:22
  293.0 6.5 %collective-permute-start.5 = (bf16[32,1536]{1,0:T(8,128)(2,1)}, bf16[32,1536]{1,0:T(8,128)(2,1)S(1)}, u32[]{:S(2)}, u32[]{:S(2)}) collective-permute-start(bf16[32,1536]{1,0:T(8,128)(2,1)} %get-tuple-element.351), channel_id=1, source_target_pairs={{0,3},{1,2},{2,1},{3,0},{4,7},{5,6},{6,5},{7,4},{8,11},{9,10},{10,... | collective-permute-start | bytes 294920 | tf_op jit(solution)/shard_map/while/body/eval_jaxpr/ppermute | solution.py:22
  293.0 8.0 %collective-permute-start.6 = (bf16[32,1536]{1,0:T(8,128)(2,1)S(1)}, bf16[32,1536]{1,0:T(8,128)(2,1)S(1)}, u32[]{:S(2)}, u32[]{:S(2)}) collective-permute-start(bf16[32,1536]{1,0:T(8,128)(2,1)S(1)} %get-tuple-element.352), channel_id=1, source_target_pairs={{0,4},{1,5},{2,6},{3,7},{4,0},{5,1},{6,2},{7,3},{8,12},{9,13},{10,... | collective-permute-start | bytes 294920 | tf_op jit(solution)/shard_map/while/body/eval_jaxpr/ppermute | solution.py:22
  295.7 9.7 %collective-permute-start.7 = (bf16[32,1536]{1,0:T(8,128)(2,1)S(1)}, bf16[32,1536]{1,0:T(8,128)(2,1)S(1)}, u32[]{:S(2)}, u32[]{:S(2)}) collective-permute-start(bf16[32,1536]{1,0:T(8,128)(2,1)S(1)} %get-tuple-element.353), channel_id=1, source_target_pairs={{0,5},{1,4},{2,7},{3,6},{4,1},{5,0},{6,3},{7,2},{8,13},{9,12},{10,... | collective-permute-start | bytes 294920 | tf_op jit(solution)/shard_map/while/body/eval_jaxpr/ppermute | solution.py:22
  296.8 8.6 %collective-permute-start.8 = (bf16[32,1536]{1,0:T(8,128)(2,1)S(1)}, bf16[32,1536]{1,0:T(8,128)(2,1)S(1)}, u32[]{:S(2)}, u32[]{:S(2)}) collective-permute-start(bf16[32,1536]{1,0:T(8,128)(2,1)S(1)} %get-tuple-element.354), channel_id=1, source_target_pairs={{0,6},{1,7},{2,4},{3,5},{4,2},{5,3},{6,0},{7,1},{8,14},{9,15},{10,... | collective-permute-start | bytes 294920 | tf_op jit(solution)/shard_map/while/body/eval_jaxpr/ppermute | solution.py:22
  299.5 6.0 %collective-permute-start.9 = (bf16[32,1536]{1,0:T(8,128)(2,1)S(1)}, bf16[32,1536]{1,0:T(8,128)(2,1)S(1)}, u32[]{:S(2)}, u32[]{:S(2)}) collective-permute-start(bf16[32,1536]{1,0:T(8,128)(2,1)S(1)} %get-tuple-element.355), channel_id=1, source_target_pairs={{0,7},{1,6},{2,5},{3,4},{4,3},{5,2},{6,1},{7,0},{8,15},{9,14},{10,... | collective-permute-start | bytes 294920 | tf_op jit(solution)/shard_map/while/body/eval_jaxpr/ppermute | solution.py:22
  (8 other events, 35.9 us)
